TPU v7x, 32 devices: a whole 2x2x4 slice. The times are simulated.
32 devices in a mesh: tm: 4 (over y, core), space: 8 (over z, x).
Axes of the slice: x: 2, y: 2, z: 4, core: 2. Of those that a mesh axis runs over, the one named last changes fastest.
Arguments:
- query_rows: bfloat16 [8192, 2560], P(('tm', 'space')), may hold values from -18 to 18
- key_rows: bfloat16 [8192, 2560], P(('tm', 'space')), may hold values from -7 to 7
- value_rows: bfloat16 [8192, 2560], P(('tm', 'space')), may hold values from -12 to 12
- out_cotangent: bfloat16 [8192, 2560], P(('tm', 'space')), may hold values from -12 to 12
- tile_slot: int32 [8192], P(('tm', 'space')), may hold values from 0 to 8191, as said below
- window_reach: int32 [4, 8, 2], P(None, 'space'), may hold values from 0 to 1, as said below
Outputs:
- attended: bfloat16 [8192, 2560], P(('tm', 'space'))
- query_grad: bfloat16 [8192, 2560], P(('tm', 'space'))
- key_grad: bfloat16 [8192, 2560], P(('tm', 'space'))
- value_grad: bfloat16 [8192, 2560], P(('tm', 'space'))
Inputs may be any that keep to these rules, and one draw needn't show every extreme that they name: `tile_slot`: A permutation of the tile-order positions. The raster tokens r * 256 to r * 256 + 256 - 1 (shard r, counted over tm first, then space) take, for every shard d, exactly the 8 positions d * 256 + r * 8 to d * 256 + r * 8 + 7. `window_reach`: entry 0 is 0 in the lowest slab and entry 1 is 0 in the highest slab.
All inputs are finite; a program needn't handle non-finite values.
Results may differ from a plain program's by a relative error of at most 0.0053.
Values may be sent and summed in bfloat16 or wider, within the bound.
A program may use at most 192 MiB of HBM per device.

v0:
```python
import jax
import jax.numpy as jnp
from jax import lax
from jax.sharding import PartitionSpec as P

H = 20
HD = 128
TILE = 256


def extended_2(cells, sides, width):
    for axis, dim in sides:
        count = lax.axis_size(axis)
        ends = count - 1
        head = lax.slice_in_dim(cells, 0, width, axis=dim)
        tail = lax.slice_in_dim(cells, cells.shape[dim] - width, cells.shape[dim], axis=dim)
        cells = jnp.concatenate(
            [
                lax.ppermute(tail, axis, [(i, (i + 1) % count) for i in range(ends)]),
                cells,
                lax.ppermute(head, axis, [((i + 1) % count, i) for i in range(ends)]),
            ],
            axis=dim,
        )
    return cells


def passed_along(block, axis, distance):
    devices = range(lax.axis_size(axis))
    route = [(i - distance, i) for i in devices if i - distance in devices]
    return lax.ppermute(block, axis, route)


def slice_channels(array, column, block_width):
    return lax.dynamic_slice_in_dim(array, column, block_width, array.ndim - 1)


def head_blocking():
    heads_block = max((divisor for divisor in range(1, 6) if H % divisor == 0))
    return (heads_block, heads_block * HD, H // heads_block)


def five_sets(extended):
    picks = [
        extended[:, 0, 1:-1],
        extended[:, 1, 1:-1],
        extended[:, 2, 1:-1],
        extended[:, 1, :-2],
        extended[:, 1, 2:],
    ]
    return jnp.stack(picks, axis=1)


def attend_all(query_tile, grad_tile, near_keys, near_values, allowed, keep_range):
    tokens_here, channels = query_tile.shape
    tiles_here = tokens_here // TILE
    sets_count = near_keys.shape[0]
    heads_block, block_width, block_count = head_blocking()
    softmax_scale = HD ** (-0.5)
    visible = allowed[:, None, None, :, None]
    keep_low, keep_high = keep_range
    terms_count = keep_high - keep_low
    shape_query = (tiles_here, TILE, heads_block, HD)
    shape_keys = (sets_count, tiles_here, TILE, heads_block, HD)
    initial = (
        jnp.zeros((tokens_here, channels), jnp.bfloat16),
        jnp.zeros((tokens_here, channels), jnp.bfloat16),
        jnp.zeros((terms_count, tokens_here, channels), jnp.float32),
        jnp.zeros((terms_count, tokens_here, channels), jnp.float32),
        jnp.zeros((3, tiles_here, H, TILE), jnp.float32),
    )

    def attend_block_step(step_index, carry):
        attended, query_grad, key_terms, value_terms, row_stats = carry
        column = step_index * block_width
        head_start = step_index * heads_block
        queries = slice_channels(query_tile, column, block_width).reshape(shape_query)
        cotangent = slice_channels(grad_tile, column, block_width).reshape(shape_query)
        keys_block = slice_channels(near_keys, column, block_width).reshape(shape_keys)
        values_block = slice_channels(near_values, column, block_width).reshape(shape_keys)
        scores = (
            jnp.einsum("tqhd,atkhd->thqak", queries, keys_block, preferred_element_type=jnp.float32)
            * softmax_scale
        )
        row_max = jnp.max(jnp.where(visible, scores, -1e30), axis=(3, 4), keepdims=True)
        expo = jnp.where(visible, jnp.exp(scores - row_max), 0.0)
        row_sum = jnp.sum(expo, axis=(3, 4), keepdims=True)
        weights = expo / row_sum
        weights_low = weights.astype(jnp.bfloat16)
        output = jnp.einsum(
            "thqak,atkhd->tqhd", weights_low, values_block, preferred_element_type=jnp.float32
        )
        dweights = jnp.einsum(
            "tqhd,atkhd->thqak", cotangent, values_block, preferred_element_type=jnp.float32
        )
        row_dot = jnp.sum(weights * dweights, axis=(3, 4), keepdims=True)
        dscores = (weights * (dweights - row_dot) * softmax_scale).astype(jnp.bfloat16)
        query_part = jnp.einsum(
            "thqak,atkhd->tqhd", dscores, keys_block, preferred_element_type=jnp.float32
        )
        key_part = jnp.einsum(
            "thqak,tqhd->atkhd",
            dscores[:, :, :, keep_low:keep_high],
            queries,
            preferred_element_type=jnp.float32,
        )
        value_part = jnp.einsum(
            "thqak,tqhd->atkhd",
            weights_low[:, :, :, keep_low:keep_high],
            cotangent,
            preferred_element_type=jnp.float32,
        )
        attended = lax.dynamic_update_slice_in_dim(
            attended, output.reshape(tokens_here, block_width).astype(jnp.bfloat16), column, 1
        )
        query_grad = lax.dynamic_update_slice_in_dim(
            query_grad, query_part.reshape(tokens_here, block_width).astype(jnp.bfloat16), column, 1
        )
        key_terms = lax.dynamic_update_slice_in_dim(
            key_terms, key_part.reshape(terms_count, tokens_here, block_width), column, 2
        )
        value_terms = lax.dynamic_update_slice_in_dim(
            value_terms, value_part.reshape(terms_count, tokens_here, block_width), column, 2
        )
        block_stats = jnp.stack([row_max, row_sum, row_dot]).reshape(
            3, tiles_here, heads_block, TILE
        )
        row_stats = lax.dynamic_update_slice_in_dim(row_stats, block_stats, head_start, 2)
        return (attended, query_grad, key_terms, value_terms, row_stats)

    return lax.fori_loop(0, block_count, attend_block_step, initial)


def neighbour_terms(near_rows, near_stats, key_tile, value_tile, includes, key_start, value_start):
    tokens_here, channels = key_tile.shape
    tiles_here = tokens_here // TILE
    heads_block, block_width, block_count = head_blocking()
    softmax_scale = HD ** (-0.5)
    shape_rows = (tiles_here, TILE, heads_block, HD)

    def neighbour_block_step(step_index, carry):
        key_total, value_total = carry
        column = step_index * block_width
        head_start = step_index * heads_block
        keys_block = slice_channels(key_tile, column, block_width).reshape(shape_rows)
        values_block = slice_channels(value_tile, column, block_width).reshape(shape_rows)
        key_sum = jnp.zeros(shape_rows, jnp.float32)
        value_sum = jnp.zeros(shape_rows, jnp.float32)
        for near_side in range(len(includes)):
            queries = slice_channels(near_rows[0, near_side], column, block_width).reshape(
                shape_rows
            )
            cotangent = slice_channels(near_rows[1, near_side], column, block_width).reshape(
                shape_rows
            )
            block_stats = lax.dynamic_slice_in_dim(
                near_stats[:, near_side], head_start, heads_block, 2
            )
            visible = includes[near_side][:, None, None, None]
            scores = (
                jnp.einsum(
                    "tqhd,tkhd->thqk", queries, keys_block, preferred_element_type=jnp.float32
                )
                * softmax_scale
            )
            safe_sum = jnp.where(visible, block_stats[1][..., None], 1.0)
            weights = jnp.where(
                visible, jnp.exp(scores - block_stats[0][..., None]) / safe_sum, 0.0
            )
            weights_low = weights.astype(jnp.bfloat16)
            dweights = jnp.einsum(
                "tqhd,tkhd->thqk", cotangent, values_block, preferred_element_type=jnp.float32
            )
            dscores = (weights * (dweights - block_stats[2][..., None]) * softmax_scale).astype(
                jnp.bfloat16
            )
            key_sum = key_sum + jnp.einsum(
                "thqk,tqhd->tkhd", dscores, queries, preferred_element_type=jnp.float32
            )
            value_sum = value_sum + jnp.einsum(
                "thqk,tqhd->tkhd", weights_low, cotangent, preferred_element_type=jnp.float32
            )
        key_total = lax.dynamic_update_slice_in_dim(
            key_total,
            slice_channels(key_total, column, block_width)
            + key_sum.reshape(tokens_here, block_width),
            column,
            1,
        )
        value_total = lax.dynamic_update_slice_in_dim(
            value_total,
            slice_channels(value_total, column, block_width)
            + value_sum.reshape(tokens_here, block_width),
            column,
            1,
        )
        return (key_total, value_total)

    key_total, value_total = lax.fori_loop(
        0, block_count, neighbour_block_step, (key_start, value_start)
    )
    return (key_total.astype(jnp.bfloat16), value_total.astype(jnp.bfloat16))


def shards(query_rows, key_rows, value_rows, out_cotangent, tile_slot, window_reach):
    tokens_here, channels = query_rows.shape
    tm_count = lax.axis_size("tm")
    space_count = lax.axis_size("space")
    per_peer = tokens_here // (tm_count * space_count)
    own_rank = lax.axis_index("tm") * space_count + lax.axis_index("space")
    landing = tile_slot // tokens_here * per_peer + tile_slot % tokens_here - own_rank * per_peer
    chosen = (
        jnp.zeros((tokens_here,), jnp.int32)
        .at[landing]
        .set(jnp.arange(tokens_here, dtype=jnp.int32))
    )
    send_query = query_rows[chosen]
    send_key = key_rows[chosen]
    send_value = value_rows[chosen]
    send_grad = out_cotangent[chosen]
    query_tile, key_tile, value_tile, grad_tile = (
        lax.all_to_all(send_query, ("tm", "space"), split_axis=0, concat_axis=0, tiled=True),
        lax.all_to_all(send_key, ("tm", "space"), split_axis=0, concat_axis=0, tiled=True),
        lax.all_to_all(send_value, ("tm", "space"), split_axis=0, concat_axis=0, tiled=True),
        lax.all_to_all(send_grad, ("tm", "space"), split_axis=0, concat_axis=0, tiled=True),
    )
    tiles_here = tokens_here // TILE
    slab_index = lax.axis_index("tm")
    column_count = space_count * tiles_here
    column_ids = lax.axis_index("space") * tiles_here + jnp.arange(tiles_here, dtype=jnp.int32)
    left_open = column_ids > 0
    right_open = column_ids < column_count - 1
    own_reach = lax.dynamic_index_in_dim(window_reach, slab_index, 0, keepdims=False)
    allowed = jnp.stack(
        [own_reach[:, 0] > 0, own_reach[:, 0] >= 0, own_reach[:, 1] > 0, left_open, right_open],
        axis=1,
    )
    tile_grid = (1, tiles_here, TILE, channels)
    stacked_pair = jnp.stack([key_tile.reshape(tile_grid), value_tile.reshape(tile_grid)])
    extended = extended_2(stacked_pair, (("tm", 1), ("space", 2)), 1)
    near_pair = five_sets(extended).reshape(2, 5, tokens_here, channels)
    keep_range = (0, 3)
    attended_tile, query_grad_tile, key_terms, value_terms, row_stats = attend_all(
        query_tile, grad_tile, near_pair[0], near_pair[1], allowed, keep_range
    )
    column_stats = extended_2(row_stats, (("space", 1),), 1)
    left_stats = column_stats[:, :-2]
    right_stats = column_stats[:, 2:]
    lower_terms = passed_along(jnp.stack([key_terms[0], value_terms[0]]), "tm", -1)
    upper_terms = passed_along(jnp.stack([key_terms[2], value_terms[2]]), "tm", 1)
    key_start = key_terms[1] + lower_terms[0] + upper_terms[0]
    value_start = value_terms[1] + lower_terms[1] + upper_terms[1]
    stacked_rows = jnp.stack(
        [
            query_tile.reshape(tiles_here, TILE, channels),
            grad_tile.reshape(tiles_here, TILE, channels),
        ]
    )
    side_halo = extended_2(stacked_rows, (("space", 1),), 1)
    side_rows = jnp.stack([side_halo[:, :-2], side_halo[:, 2:]], axis=1).reshape(
        2, 2, tokens_here, channels
    )
    side_stats = jnp.stack([left_stats, right_stats], axis=1)
    key_grad_tile, value_grad_tile = neighbour_terms(
        side_rows, side_stats, key_tile, value_tile, (left_open, right_open), key_start, value_start
    )
    back_rows = (
        lax.all_to_all(attended_tile, ("tm", "space"), split_axis=0, concat_axis=0, tiled=True),
        lax.all_to_all(query_grad_tile, ("tm", "space"), split_axis=0, concat_axis=0, tiled=True),
        lax.all_to_all(key_grad_tile, ("tm", "space"), split_axis=0, concat_axis=0, tiled=True),
        lax.all_to_all(value_grad_tile, ("tm", "space"), split_axis=0, concat_axis=0, tiled=True),
    )
    return (
        back_rows[0][landing],
        back_rows[1][landing],
        back_rows[2][landing],
        back_rows[3][landing],
    )


def solution(mesh):
    return jax.shard_map(
        shards,
        mesh=mesh,
        in_specs=(
            P(("tm", "space"), None),
            P(("tm", "space"), None),
            P(("tm", "space"), None),
            P(("tm", "space"), None),
            P(("tm", "space")),
            P(None, "space", None),
        ),
        out_specs=(
            P(("tm", "space"), None),
            P(("tm", "space"), None),
            P(("tm", "space"), None),
            P(("tm", "space"), None),
        ),
        check_vma=False,
    )
```

profile of v0, /device:TPU:0, one launch (start us, length us, event | category | flops | bytes accessed | tf_op | source)
XLA Modules:
  0.0 1009.7 jit_solution(15235539556442133887)
XLA Ops:
  5.4 7.4 all-to-all-start.1
  14.3 31.7 %all-to-all-done.1 = bf16[32,8,2560]{2,1,0:T(8,128)(2,1)} async-done(((bf16[32,8,2560]{2,1,0:T(8,128)(2,1)}), bf16[32,8,2560]{2,1,0:T(8,128)(2,1)}, u32[]{:S(2)}, u32[]{:S(2)}) %all-to-all-start.1) | async-done | bytes 1310752 | tf_op jit(solution)/shard_map/all_to_all | solution.py:224
  46.0 35.6 %all_to_all.96 = bf16[32,8,2560]{2,1,0:T(8,128)(2,1)} all-to-all(bf16[32,8,2560]{2,1,0:T(8,128)(2,1)S(1)} %bitcast.292), channel_id=1, replica_groups=mesh['tm'=4,'space'=8] {'tm','space'}, dimensions={0} | all-to-all | bytes 2621440 | tf_op jit(solution)/shard_map/all_to_all | solution.py:223
  92.5 6.0 pad_maximum_fusion
  98.5 6.1 collective-permute-start.2
  108.4 29.5 %all-to-all-start.2 = ((bf16[32,8,2560]{2,1,0:T(8,128)(2,1)}), bf16[32,8,2560]{2,1,0:T(8,128)(2,1)S(1)}, u32[]{:S(2)}, u32[]{:S(2)}) async-start(bf16[32,8,2560]{2,1,0:T(8,128)(2,1)} %bitcast.290), calls=%async_computation.2 | async-start | bytes 2621440 | tf_op jit(solution)/shard_map/all_to_all | solution.py:222
  152.0 297.5 %all-to-all-done.2 = bf16[32,8,2560]{2,1,0:T(8,128)(2,1)S(1)} async-done(((bf16[32,8,2560]{2,1,0:T(8,128)(2,1)}), bf16[32,8,2560]{2,1,0:T(8,128)(2,1)S(1)}, u32[]{:S(2)}, u32[]{:S(2)}) %all-to-all-start.2) | async-done | bytes 1310752 | tf_op jit(solution)/shard_map/all_to_all | solution.py:222
  449.6 8.9 all-to-all-start.3
  465.3 9.5 slice_bitcast_fusion.8
  474.8 16.7 %all-to-all-done.3 = bf16[32,8,2560]{2,1,0:T(8,128)(2,1)S(1)} async-done(((bf16[32,8,2560]{2,1,0:T(8,128)(2,1)}), bf16[32,8,2560]{2,1,0:T(8,128)(2,1)S(1)}, u32[]{:S(2)}, u32[]{:S(2)}) %all-to-all-start.3) | async-done | bytes 1310752 | tf_op jit(solution)/shard_map/all_to_all | solution.py:225
  501.2 172.5 %while.36 = (s32[]{:T(128)}, bf16[256,2560]{1,0:T(8,128)(2,1)}, bf16[256,2560]{1,0:T(8,128)(2,1)}, f32[3,256,2560]{1,2,0:T(8,128)}, f32[3,256,2560]{1,2,0:T(8,12...) while((s32[]{:T(128)}, bf16[256,2560]{1,0:T(8,128)(2,1)}, ...), condition=%wide.region_5.6_spmd, body=%wide.region_1.5_spmd.sunk | while | flops 2217414400 | bytes 196060720 | solution.py:131
  563.9 5.2 multiply_reduce_fusion.2
  693.0 6.1 collective-permute-start.6
  702.0 62.0 %collective-permute-done.7 = bf16[2,1,256,2560]{3,2,1,0:T(8,128)(2,1)} collective-permute-done((bf16[2,1,256,2560]{3,2,1,0:T(8,128)(2,1)}, bf16[2,1,256,2560]{3,2,1,0:T(8,128)(2,1)}, u32[]{:S(2)}, u32[]{:S(2)}) %collective-permute-start.7) | collective-permute-done | bytes 2621472 | tf_op jit(solution)/shard_map/ppermute | solution.py:21
  764.0 55.9 %collective-permute-done.6 = bf16[2,1,256,2560]{3,2,0,1:T(8,128)(2,1)} collective-permute-done((bf16[2,1,256,2560]{3,2,0,1:T(8,128)(2,1)}, bf16[2,1,256,2560]{3,2,0,1:T(8,128)(2,1)}, u32[]{:S(2)}, u32[]{:S(2)}) %collective-permute-start.6) | collective-permute-done | bytes 2621472 | tf_op jit(solution)/shard_map/ppermute | solution.py:19
  819.9 5.4 maximum_bitcast_fusion.1
  825.3 8.0 copy.124
  839.0 8.9 fusion.55
  852.1 73.8 %while.37 = (s32[]{:T(128)}, f32[256,2560]{0,1:T(8,128)}, f32[256,2560]{0,1:T(8,128)}, bf16[2,2,256,2560]{2,3,1,0:T(8,128)(2,1)}, pred[1]{0:T(512)(128)(4,1)}, /...) while((s32[]{:T(128)}, f32[256,2560]{0,1:T(8,128)}, ...), condition=%wide.region_7.8_spmd, body=%wide.region_6.7_spmd.sunk | while | flops 677644800 | bytes 40724916 | solution.py:199
  928.7 5.8 all-to-all-start.6
  937.4 30.3 %all-to-all-done.6 = bf16[32,8,2560]{2,1,0:T(8,128)(2,1)S(1)} async-done(((bf16[32,8,2560]{2,1,0:T(8,128)(2,1)}), bf16[32,8,2560]{2,1,0:T(8,128)(2,1)S(1)}, u32[]{:S(2)}, u32[]{:S(2)}) %all-to-all-start.6) | async-done | bytes 1310752 | tf_op jit(solution)/shard_map/all_to_all | solution.py:270
  973.9 5.3 gather_fusion.5
  981.7 22.6 %all-to-all-done.7 = bf16[32,8,2560]{2,1,0:T(8,128)(2,1)} async-done(((bf16[32,8,2560]{2,1,0:T(8,128)(2,1)}), bf16[32,8,2560]{2,1,0:T(8,128)(2,1)}, u32[]{:S(2)}, u32[]{:S(2)}) %all-to-all-start.7) | async-done | bytes 1310752 | tf_op jit(solution)/shard_map/all_to_all | solution.py:271
  1004.3 5.4 gather_fusion.7
  (342 shorter events, 335.8 us)
Async XLA Ops:
  5.4 7.4 copy-start.7
  5.4 40.6 %all-to-all-start.1 = ((bf16[32,8,2560]{2,1,0:T(8,128)(2,1)}), bf16[32,8,2560]{2,1,0:T(8,128)(2,1)}, u32[]{:S(2)}, u32[]{:S(2)}) async-start(bf16[32,8,2560]{2,1,0:T(8,128)(2,1)} %bitcast.55), calls=%async_computation.1 | async-start | bytes 2621440 | tf_op jit(solution)/shard_map/all_to_all | solution.py:224
  83.6 5.8 collective-permute-start
  85.0 7.4 collective-permute-start.1
  89.4 9.1 copy-start.17
  92.5 13.4 %copy-start.8 = (bf16[256,2560]{1,0:T(8,128)(2,1)S(1)}, bf16[256,2560]{1,0:T(8,128)(2,1)}, u32[]{:S(2)}) copy-start(bf16[256,2560]{1,0:T(8,128)(2,1)} %param.10) | copy-start | bytes 3932164
  98.5 360.0 %collective-permute-start.2 = (bf16[2,3,1,256,2560]{4,3,2,1,0:T(8,128)(2,1)}, bf16[2,3,1,256,2560]{4,3,2,1,0:T(8,128)(2,1)}, u32[]{:S(2)}, u32[]{:S(2)}) collective-permute-start(bf16[2,3,1,256,2560]{4,3,2,1,0:T(8,128)(2,1)} %pad_maximum_fusion), channel_id=1, source_target_pairs={{0,1},{1,2},{2,3},{3,4},{4,5},{5,6},{6,7},{8,9},{9,10},{10,11},{11... | collective-permute-start | bytes 23592968 | tf_op jit(solution)/shard_map/ppermute | solution.py:19
  104.6 357.2 %collective-permute-start.3 = (bf16[2,3,1,256,2560]{4,3,2,1,0:T(8,128)(2,1)}, bf16[2,3,1,256,2560]{4,3,2,1,0:T(8,128)(2,1)}, u32[]{:S(2)}, u32[]{:S(2)}) collective-permute-start(bf16[2,3,1,256,2560]{4,3,2,1,0:T(8,128)(2,1)} %pad_maximum_fusion), channel_id=1, source_target_pairs={{1,0},{2,1},{3,2},{4,3},{5,4},{6,5},{7,6},{9,8},{10,9},{11,10},{12... | collective-permute-start | bytes 23592968 | tf_op jit(solution)/shard_map/ppermute | solution.py:21
  108.4 29.6 %copy-start.23 = (s32[4,1,2]{0,2,1:T(2,128)S(1)}, s32[4,1,2]{0,2,1:T(2,128)}, u32[]{:S(2)}) copy-start(s32[4,1,2]{0,2,1:T(2,128)} %param.15) | copy-start | bytes 100
  108.4 32.3 %copy-start.9 = (bf16[256,2560]{1,0:T(8,128)(2,1)S(1)}, bf16[256,2560]{1,0:T(8,128)(2,1)}, u32[]{:S(2)}) copy-start(bf16[256,2560]{1,0:T(8,128)(2,1)} %param.13) | copy-start | bytes 3932164
  108.4 341.2 %all-to-all-start.2 = ((bf16[32,8,2560]{2,1,0:T(8,128)(2,1)}), bf16[32,8,2560]{2,1,0:T(8,128)(2,1)S(1)}, u32[]{:S(2)}, u32[]{:S(2)}) async-start(bf16[32,8,2560]{2,1,0:T(8,128)(2,1)} %bitcast.290), calls=%async_computation.2 | async-start | bytes 2621440 | tf_op jit(solution)/shard_map/all_to_all | solution.py:222
  449.6 41.9 %all-to-all-start.3 = ((bf16[32,8,2560]{2,1,0:T(8,128)(2,1)}), bf16[32,8,2560]{2,1,0:T(8,128)(2,1)S(1)}, u32[]{:S(2)}, u32[]{:S(2)}) async-start(bf16[32,8,2560]{2,1,0:T(8,128)(2,1)} %bitcast.291), calls=%async_computation.3 | async-start | bytes 2621440 | tf_op jit(solution)/shard_map/all_to_all | solution.py:225
  681.2 157.8 %collective-permute-start.5 = (f32[2,256,2560]{1,2,0:T(8,128)}, f32[2,256,2560]{1,2,0:T(8,128)}, u32[]{:S(2)}, u32[]{:S(2)}) collective-permute-start(f32[2,256,2560]{1,2,0:T(8,128)} %pad_maximum_fusion.2), channel_id=1, source_target_pairs={{0,8},{8,16},{16,24},{1,9},{9,17},{17,25},{2,10},{10,18},{18,26},{... | collective-permute-start | bytes 15728648 | tf_op jit(solution)/shard_map/ppermute | solution.py:31
  687.8 151.2 %collective-permute-start.4 = (f32[2,256,2560]{1,2,0:T(8,128)}, f32[2,256,2560]{1,2,0:T(8,128)}, u32[]{:S(2)}, u32[]{:S(2)}) collective-permute-start(f32[2,256,2560]{1,2,0:T(8,128)} %pad_maximum_fusion.1), channel_id=1, source_target_pairs={{8,0},{16,8},{24,16},{9,1},{17,9},{25,17},{10,2},{18,10},{26,18},{... | collective-permute-start | bytes 15728648 | tf_op jit(solution)/shard_map/ppermute | solution.py:31
  691.7 72.3 %collective-permute-start.7 = (bf16[2,1,256,2560]{3,2,1,0:T(8,128)(2,1)}, bf16[2,1,256,2560]{3,2,1,0:T(8,128)(2,1)}, u32[]{:S(2)}, u32[]{:S(2)}) collective-permute-start(bf16[2,1,256,2560]{3,2,1,0:T(8,128)(2,1)} %get-tuple-element.512), channel_id=1, source_target_pairs={{1,0},{2,1},{3,2},{4,3},{5,4},{6,5},{7,6},{9,8},{10,9},{11,10},{12... | collective-permute-start | bytes 7864328 | tf_op jit(solution)/shard_map/ppermute | solution.py:21
  693.0 127.0 %collective-permute-start.6 = (bf16[2,1,256,2560]{3,2,0,1:T(8,128)(2,1)}, bf16[2,1,256,2560]{3,2,0,1:T(8,128)(2,1)}, u32[]{:S(2)}, u32[]{:S(2)}) collective-permute-start(bf16[2,1,256,2560]{3,2,0,1:T(8,128)(2,1)} %get-tuple-element.511), channel_id=1, source_target_pairs={{0,1},{1,2},{2,3},{3,4},{4,5},{5,6},{6,7},{8,9},{9,10},{10,11},{11... | collective-permute-start | bytes 7864328 | tf_op jit(solution)/shard_map/ppermute | solution.py:19
  699.1 148.9 %all-to-all-start.4 = ((bf16[32,8,2560]{2,1,0:T(8,128)(2,1)}), bf16[32,8,2560]{2,1,0:T(8,128)(2,1)S(1)}, u32[]{:S(2)}, u32[]{:S(2)}) async-start(bf16[32,8,2560]{2,1,0:T(8,128)(2,1)} %bitcast.293), calls=%async_computation.4 | async-start | bytes 2621440 | tf_op jit(solution)/shard_map/all_to_all | solution.py:268
  833.3 18.7 %collective-permute-start.8 = (f32[3,1,20,256]{3,2,1,0:T(8,128)S(1)}, f32[3,1,20,256]{3,2,1,0:T(8,128)S(1)}, u32[]{:S(2)}, u32[]{:S(2)}) collective-permute-start(f32[3,1,20,256]{3,2,1,0:T(8,128)S(1)} %bitcast.303), channel_id=1, source_target_pairs={{0,1},{1,2},{2,3},{3,4},{4,5},{5,6},{6,7},{8,9},{9,10},{10,11},{11... | collective-permute-start | bytes 184328 | tf_op jit(solution)/shard_map/ppermute | solution.py:19
  837.7 14.4 %collective-permute-start.9 = (f32[3,1,20,256]{3,2,1,0:T(8,128)S(1)}, f32[3,1,20,256]{3,2,1,0:T(8,128)S(1)}, u32[]{:S(2)}, u32[]{:S(2)}) collective-permute-start(f32[3,1,20,256]{3,2,1,0:T(8,128)S(1)} %bitcast.304), channel_id=1, source_target_pairs={{1,0},{2,1},{3,2},{4,3},{5,4},{6,5},{7,6},{9,8},{10,9},{11,10},{12... | collective-permute-start | bytes 184328 | tf_op jit(solution)/shard_map/ppermute | solution.py:21
  848.0 80.7 %all-to-all-start.5 = ((bf16[32,8,2560]{2,1,0:T(8,128)(2,1)}), bf16[32,8,2560]{2,1,0:T(8,128)(2,1)}, u32[]{:S(2)}, u32[]{:S(2)}) async-start(bf16[32,8,2560]{2,1,0:T(8,128)(2,1)} %bitcast.68), calls=%async_computation.5 | async-start | bytes 2621440 | tf_op jit(solution)/shard_map/all_to_all | solution.py:269
  928.7 39.0 %all-to-all-start.6 = ((bf16[32,8,2560]{2,1,0:T(8,128)(2,1)}), bf16[32,8,2560]{2,1,0:T(8,128)(2,1)S(1)}, u32[]{:S(2)}, u32[]{:S(2)}) async-start(bf16[32,8,2560]{2,1,0:T(8,128)(2,1)} %bitcast.141), calls=%async_computation.6 | async-start | bytes 2621440 | tf_op jit(solution)/shard_map/all_to_all | solution.py:270
  934.5 36.9 %copy-start.22 = (s32[256]{0:T(256)S(1)}, s32[256]{0:T(256)}, u32[]{:S(2)}) copy-start(s32[256]{0:T(256)} %copy-done.21) | copy-start | bytes 3076
  934.5 36.9 %copy-start.6 = (bf16[32,8,2560]{2,1,0:T(8,128)(2,1)S(1)}, bf16[32,8,2560]{2,1,0:T(8,128)(2,1)}, u32[]{:S(2)}) copy-start(bf16[32,8,2560]{2,1,0:T(8,128)(2,1)} %copy-done.5) | copy-start | bytes 3932164
  967.7 36.6 %all-to-all-start.7 = ((bf16[32,8,2560]{2,1,0:T(8,128)(2,1)}), bf16[32,8,2560]{2,1,0:T(8,128)(2,1)}, u32[]{:S(2)}, u32[]{:S(2)}) async-start(bf16[32,8,2560]{2,1,0:T(8,128)(2,1)} %bitcast.294), calls=%async_computation.7 | async-start | bytes 2621440 | tf_op jit(solution)/shard_map/all_to_all | solution.py:271
  (58 other events, 175.1 us)
where the time goes:
time: 1010 us
  waiting for transfers between devices  523 us (52%)
  local copies, waits for them, and re-layouts  202 us (20%)
  starting transfers between devices  90.6 us (9%)
  matrix products  82.1 us (8%)
  other arithmetic  72.5 us (7%)
  blocking collectives  35.6 us (4%)
    all_to_all x1, waiting for transfers between devices, shards(): lax.all_to_all(send_query, ('tm', 'space'), split_axis=0, concat_axis=0,...  298 us
    dynamic_slice x52, local copies, waits for them, and re-layouts, slice_channels(): return lax.dynamic_slice_in_dim(array, column, block_width, array.ndim - 1)  68.1 us
    ppermute x4, waiting for transfers between devices, extended_2(): lax.ppermute(head, axis, [((i + 1) % count, i) for i in range(ends)])  65.1 us
    ppermute x4, waiting for transfers between devices, extended_2(): lax.ppermute(tail, axis, [(i, (i + 1) % count) for i in range(ends)])  59 us
    all_to_all x1, blocking collectives, shards(): lax.all_to_all(send_key, ('tm', 'space'), split_axis=0, concat_axis=0, ti...  35.6 us
    all_to_all x1, waiting for transfers between devices, shards(): lax.all_to_all(send_value, ('tm', 'space'), split_axis=0, concat_axis=0,...  31.7 us
    all_to_all x1, waiting for transfers between devices, shards(): lax.all_to_all(key_grad_tile, ('tm', 'space'), split_axis=0, concat_axis=...  30.3 us
    all_to_all x1, starting transfers between devices, shards(): lax.all_to_all(send_query, ('tm', 'space'), split_axis=0, concat_axis=0,...  29.5 us
  transfers between devices with their start and end apart: 17, of which 9 were waited for; matrix products, arithmetic and copies ran while one was open for 15% of the time, Pallas kernels for 0%

commit v1 on v0

v1 whole, which is shorter than its diff:
```python
import functools
import math

import jax
import jax.numpy as jnp
from jax import lax
from jax.experimental import pallas as pl
from jax.experimental.pallas import tpu as pltpu
from jax.sharding import PartitionSpec as P

H = 20
HD = 128
TILE = 256
PAIR = 2 * HD
CHUNKS = 2
BOTH = ("tm", "space")
SCALE = HD ** (-0.5)
VMEM_LIMIT = 40 * 1024 * 1024


def device_of(tile, tm_count, space_count):
    if (tm_count, space_count) != (4, 8):
        return tile
    slab, column = tile // 8, tile % 8
    z, core = column // 2, column % 2
    y = slab // 2
    x = (slab + y) % 2
    return (y * 2 + core) * 8 + z * 2 + x


def tile_of(rank, tm_count, space_count):
    if (tm_count, space_count) != (4, 8):
        return rank
    tm, space = rank // 8, rank % 8
    y, core = tm // 2, tm % 2
    z, x = space // 2, space % 2
    return (y * 2 + (x + y) % 2) * 8 + z * 2 + core


def dot(a, b, dims):
    return lax.dot_general(a, b, (dims, ((), ())), preferred_element_type=jnp.float32)


def pack_body(landing_ref, q_ref, k_ref, v_ref, g_ref, kv_ref, qg_ref):
    rows = lax.broadcasted_iota(jnp.int32, (TILE, TILE), 0)
    pick = jnp.where(rows == landing_ref[...], 1.0, 0.0).astype(jnp.bfloat16)
    for ref, out, at in ((k_ref, kv_ref, 0), (v_ref, kv_ref, 1), (q_ref, qg_ref, 0), (g_ref, qg_ref, 1)):
        moved = dot(pick, ref[...], ((1,), (0,)))
        out[:, at * PAIR : (at + 1) * PAIR] = moved.astype(jnp.bfloat16)


def pack(landing, arrays, chunk, steps):
    width = steps * 2 * PAIR
    rows = arrays[0].shape[0]
    source = pl.BlockSpec((rows, PAIR), lambda i: (0, chunk * steps + i))
    target = pl.BlockSpec((rows, 2 * PAIR), lambda i: (0, i))
    shape = jax.ShapeDtypeStruct((rows, width), jnp.bfloat16)
    return pl.pallas_call(
        pack_body,
        grid=(steps,),
        in_specs=[pl.BlockSpec((1, rows), lambda i: (0, 0))] + [source] * 4,
        out_specs=[target] * 2,
        out_shape=[shape] * 2,
        cost_estimate=pl.CostEstimate(
            flops=4 * rows * rows * width, bytes_accessed=8 * rows * width, transcendentals=0
        ),
        name="pack",
    )(landing[None, :], *arrays)


def unpack_body(steps, landing_ref, *refs):
    chunk_refs, (first_ref, second_ref) = refs[:-2], refs[-2:]
    columns = lax.broadcasted_iota(jnp.int32, (TILE, TILE), 1)
    pick = jnp.where(columns == landing_ref[...], 1.0, 0.0).astype(jnp.bfloat16)
    step = pl.program_id(0)
    for chunk, ref in enumerate(chunk_refs):

        @pl.when(step // steps == chunk)
        def _(ref=ref):
            moved = dot(pick, ref[...], ((1,), (0,))).astype(jnp.bfloat16)
            first_ref[...] = moved[:, :PAIR]
            second_ref[...] = moved[:, PAIR:]


def unpack(landing, chunks, steps):
    rows = chunks[0].shape[0]
    total = steps * len(chunks)
    specs = [
        pl.BlockSpec(
            (rows, 2 * PAIR), lambda i, c=c: (0, jnp.clip(i - c * steps, 0, steps - 1))
        )
        for c in range(len(chunks))
    ]
    shape = jax.ShapeDtypeStruct((rows, total * PAIR), jnp.bfloat16)
    return pl.pallas_call(
        functools.partial(unpack_body, steps),
        grid=(total,),
        in_specs=[pl.BlockSpec((rows, 1), lambda i: (0, 0))] + specs,
        out_specs=[pl.BlockSpec((rows, PAIR), lambda i: (0, i))] * 2,
        out_shape=[shape] * 2,
        cost_estimate=pl.CostEstimate(
            flops=4 * rows * rows * total * PAIR,
            bytes_accessed=8 * rows * total * PAIR,
            transcendentals=0,
        ),
        name="unpack",
    )(landing[:, None], *chunks)


def attend_body(bias_ref, qg_ref, *refs):
    kv_refs, od_ref, own_ref, side_refs = refs[:5], refs[5], refs[6], refs[7:]
    to_log2 = SCALE * math.log2(math.e)
    for head in range(2):
        low = pl.ds(head * HD, HD)
        high = pl.ds(PAIR + head * HD, HD)
        queries, cotangent = qg_ref[:, low], qg_ref[:, high]
        scores = []
        for near, kv in enumerate(kv_refs):
            block = dot(kv[:, low], queries, ((1,), (1,))) * to_log2
            scores.append(block if near == 0 else block + bias_ref[near - 1])
        row_max = functools.reduce(
            jnp.maximum, [jnp.max(block, axis=0, keepdims=True) for block in scores]
        )
        expo = [jnp.exp2(block - row_max) for block in scores]
        row_sum = sum(jnp.sum(block, axis=0, keepdims=True) for block in expo)
        inverse = 1.0 / row_sum
        weights = [block * inverse for block in expo]
        dweights = [dot(kv[:, high], cotangent, ((1,), (1,))) for kv in kv_refs]
        row_dot = sum(
            jnp.sum(w * d, axis=0, keepdims=True) for w, d in zip(weights, dweights)
        )
        output = jnp.zeros((HD, TILE), jnp.float32)
        query_part = jnp.zeros((HD, TILE), jnp.float32)
        for near, kv in enumerate(kv_refs):
            weights_low = weights[near].astype(jnp.bfloat16)
            dscores = (weights[near] * (dweights[near] - row_dot)).astype(jnp.bfloat16)
            output += dot(kv[:, high], weights_low, ((0,), (0,)))
            query_part += dot(kv[:, low], dscores, ((0,), (0,)))
            key_term = dot(dscores, queries, ((1,), (0,))) * SCALE
            value_term = dot(weights_low, cotangent, ((1,), (0,)))
            target = own_ref if near == 0 else side_refs[near - 1]
            target[:, low] = key_term.astype(target.dtype)
            target[:, high] = value_term.astype(target.dtype)
        od_ref[:, low] = output.T.astype(jnp.bfloat16)
        od_ref[:, high] = (query_part * SCALE).T.astype(jnp.bfloat16)


def attend(bias, qg, kvs, steps):
    rows, width = qg.shape
    block = pl.BlockSpec((rows, 2 * PAIR), lambda i: (0, i))
    low = jax.ShapeDtypeStruct((rows, width), jnp.bfloat16)
    full = jax.ShapeDtypeStruct((rows, width), jnp.float32)
    heads = steps * 2
    return pl.pallas_call(
        attend_body,
        grid=(steps,),
        in_specs=[pl.BlockSpec(memory_space=pltpu.SMEM)] + [block] * 6,
        out_specs=[block] * 6,
        out_shape=[low, full, low, low, low, low],
        compiler_params=pltpu.CompilerParams(vmem_limit_bytes=VMEM_LIMIT),
        cost_estimate=pl.CostEstimate(
            flops=3 * heads * 6 * 5 * 2 * rows * rows * HD,
            bytes_accessed=13 * rows * width * 2,
            transcendentals=heads * 5 * rows * rows,
        ),
        name="attend",
    )(bias, qg, *kvs)


def shards(query_rows, key_rows, value_rows, out_cotangent, tile_slot, window_reach):
    tokens_here, channels = query_rows.shape
    tm_count = lax.axis_size("tm")
    space_count = lax.axis_size("space")
    device_count = tm_count * space_count
    per_peer = tokens_here // device_count
    slab, space = lax.axis_index("tm"), lax.axis_index("space")
    rank = slab * space_count + space
    steps = channels // PAIR // CHUNKS
    owner = functools.partial(device_of, tm_count=tm_count, space_count=space_count)

    def passed(block, slab_move, column_move):
        pairs = []
        for tile in range(device_count):
            to_slab = tile // space_count + slab_move
            to_column = tile % space_count + column_move
            if 0 <= to_slab < tm_count and 0 <= to_column < space_count:
                pairs.append((owner(tile), owner(to_slab * space_count + to_column)))
        return lax.ppermute(block, BOTH, pairs)

    landing = owner(tile_slot // tokens_here) * per_peer + tile_slot % tokens_here - rank * per_peer

    reach = lax.dynamic_index_in_dim(window_reach, slab, 0, keepdims=False)[0]
    reach = lax.ppermute(reach, BOTH, [(tile, owner(tile)) for tile in range(device_count)])
    column = tile_of(rank, tm_count, space_count) % space_count
    open_sides = jnp.stack([reach[0] > 0, reach[1] > 0, column > 0, column < space_count - 1])
    bias = jnp.where(open_sides, 0.0, -1e30).astype(jnp.float32)

    def exchange(rows):
        return lax.all_to_all(rows, BOTH, split_axis=0, concat_axis=0, tiled=True)

    moves = ((1, 0), (-1, 0), (0, 1), (0, -1))
    arrays = (query_rows, key_rows, value_rows, out_cotangent)
    back_outputs, back_terms = [], []
    for chunk in range(CHUNKS):
        send_kv, send_qg = pack(landing, arrays, chunk, steps)
        kv = exchange(send_kv)
        qg = exchange(send_qg)
        kvs = [kv] + [passed(kv, *move) for move in moves]
        outputs, own, *sides = attend(bias, qg, kvs, steps)
        back_outputs.append(exchange(outputs))
        terms = [passed(side, -a, -b) for side, (a, b) in zip(sides, moves)]
        total = own + sum(term.astype(jnp.float32) for term in terms)
        back_terms.append(exchange(total.astype(jnp.bfloat16)))
    attended, query_grad = unpack(landing, back_outputs, steps)
    key_grad, value_grad = unpack(landing, back_terms, steps)
    return (attended, query_grad, key_grad, value_grad)


def solution(mesh):
    rows = P(BOTH, None)
    return jax.shard_map(
        shards,
        mesh=mesh,
        in_specs=(rows, rows, rows, rows, P(BOTH), P(None, "space", None)),
        out_specs=(rows, rows, rows, rows),
        check_vma=False,
    )
```

time: 1010 us -> 376 us (0.37)
  waiting for transfers between devices: 523 us -> 157 us
  local copies, waits for them, and re-layouts: 202 us -> 14.7 us
  matrix products: 82.1 us -> 0 us
  other arithmetic: 72.5 us -> 8.52 us
  Pallas kernels: 0 us -> 62.6 us
    all_to_all x7, waiting for transfers between devices: 399 us -> 86.5 us  [exchange(): return lax.all_to_all(rows, BOTH, split_axis=0, concat_axis=0, tiled=True)]
    dot_general x48 -> x0, matrix products: 82.1 us -> none  [the longest x4 20.6 us: attend_block_step(): jnp.einsum('tqhd,atkhd->thqak', cotangent, values_block, preferred_elemen...]
    dynamic_slice x53 -> x1, local copies, waits for them, and re-layouts: 68.3 us -> 0.19 us  [shards(): reach = lax.dynamic_index_in_dim(window_reach, slab, 0, keepdims=False)[0]]
    pallas_call x0 -> x6, Pallas kernels: none -> 62.6 us  [the longest x2 35.2 us: attend(): pl.pallas_call(attend_body, grid=(steps,), in_specs=[pl.BlockSpec(memory_...]
    ppermute x10 -> x17, waiting for transfers between devices: 124 us -> 70.7 us  [the longest x16 70.7 us: passed(): return lax.ppermute(block, BOTH, pairs)]
    while x107 -> x0, local copies, waits for them, and re-layouts: 37.2 us -> none
    all_to_all x7, starting transfers between devices: 62.3 us -> 29.8 us  [exchange(): return lax.all_to_all(rows, BOTH, split_axis=0, concat_axis=0, tiled=True)]
    ppermute x10 -> x17, starting transfers between devices: 28.4 us -> 58.1 us  [the longest x16 57.5 us: passed(): return lax.ppermute(block, BOTH, pairs)]
  transfers between devices with their start and end apart: 17 -> 24, of which waited for: 9 -> 7; matrix products, arithmetic and copies ran while one was open for 15% -> 2% of each run, Pallas kernels for 0% -> 13%
where the time goes in v1:
time: 376 us; the launch traced here: 374 us
  waiting for transfers between devices  157 us (42%)
  starting transfers between devices  87.9 us (23%)
  Pallas kernels  62.6 us (17%)
  blocking collectives  40.5 us (11%)
  local copies, waits for them, and re-layouts  14.7 us (4%)
  other arithmetic  8.52 us (2%)
    all_to_all x7, waiting for transfers between devices, exchange(): return lax.all_to_all(rows, BOTH, split_axis=0, concat_axis=0, tiled=True)  86.5 us
    ppermute x16, waiting for transfers between devices, passed(): return lax.ppermute(block, BOTH, pairs)  70.7 us
    ppermute x16, starting transfers between devices, passed(): return lax.ppermute(block, BOTH, pairs)  57.5 us
    all_to_all x1, blocking collectives, exchange(): return lax.all_to_all(rows, BOTH, split_axis=0, concat_axis=0, tiled=True)  40.5 us
    pallas_call x2, Pallas kernels, attend(): pl.pallas_call(attend_body, grid=(steps,), in_specs=[pl.BlockSpec(memory_...  35.2 us
    all_to_all x7, starting transfers between devices, exchange(): return lax.all_to_all(rows, BOTH, split_axis=0, concat_axis=0, tiled=True)  29.8 us
    pallas_call x2, Pallas kernels, unpack(): pl.pallas_call(functools.partial(unpack_body, steps), grid=(total,), in_s...  16.6 us
    unnamed x38, local copies, waits for them, and re-layouts  13.1 us
  transfers between devices with their start and end apart: 24, of which 7 were waited for; matrix products, arithmetic and copies ran while one was open for 2% of the time, Pallas kernels for 13%

profile of v1, /device:TPU:0, one launch (start us, length us, event | category | flops | bytes accessed | tf_op | source)
XLA Modules:
  0.0 373.9 jit_solution(10559516108196781094)
XLA Ops:
  1.9 5.4 %pack.3 = (bf16[256,2560]{1,0:T(8,128)(2,1)}, bf16[256,2560]{1,0:T(8,128)(2,1)}) custom-call(s32[1,256]{1,0:T(1,128)} %bitcast.39, bf16[256,2560]{1,0:T(8,128)(2,1)} %q_ref.3, bf16[256,2560]{1,0:T(8,128)(2,1)} %k_ref.3, bf16[256,2560]{1,0:T(8,128)(2,1)} %v_ref.3, bf16[256,2560]{1,0:T(8,128)(2,1)} %g_ref.3), custom_call_target="tpu_custom_call" | custom-call | flops 671088640 | bytes 5242880 | tf_op jit(solution)/shard_map/pack/pallas_call | solution.py:58
  7.3 40.5 %all_to_all.88 = bf16[32,8,2560]{2,1,0:T(8,128)(2,1)S(1)} all-to-all(bf16[32,8,2560]{2,1,0:T(8,128)(2,1)} %bitcast.38), channel_id=1, replica_groups=mesh['tm'=4,'space'=8] {'tm','space'}, dimensions={0} | all-to-all | bytes 2621440 | tf_op jit(solution)/shard_map/all_to_all | solution.py:199
  50.5 5.4 %pack.2 = (bf16[256,2560]{1,0:T(8,128)(2,1)}, bf16[256,2560]{1,0:T(8,128)(2,1)}) custom-call(s32[1,256]{1,0:T(1,128)} %bitcast.40, bf16[256,2560]{1,0:T(8,128)(2,1)} %q_ref.3, bf16[256,2560]{1,0:T(8,128)(2,1)} %k_ref.3, bf16[256,2560]{1,0:T(8,128)(2,1)} %v_ref.3, bf16[256,2560]{1,0:T(8,128)(2,1)} %g_ref.3), custom_call_target="tpu_custom_call" | custom-call | flops 671088640 | bytes 5242880 | tf_op jit(solution)/shard_map/pack/pallas_call | solution.py:58
  55.9 27.8 %all-to-all-done.3 = bf16[32,8,2560]{2,1,0:T(8,128)(2,1)S(1)} async-done(((bf16[32,8,2560]{2,1,0:T(8,128)(2,1)}), bf16[32,8,2560]{2,1,0:T(8,128)(2,1)S(1)}, u32[]{:S(2)}, u32[]{:S(2)}) %all-to-all-start.3) | async-done | bytes 1310752 | tf_op jit(solution)/shard_map/all_to_all | solution.py:199
  87.4 4.6 %collective-permute-start.5 = (bf16[256,2560]{1,0:T(8,128)(2,1)S(1)}, bf16[256,2560]{1,0:T(8,128)(2,1)}, u32[]{:S(2)}, u32[]{:S(2)}) collective-permute-start(bf16[256,2560]{1,0:T(8,128)(2,1)S(1)} %bitcast.27), channel_id=1, source_target_pairs={{0,1},{8,9},{2,3},{10,11},{4,5},{12,13},{6,7},{14,15},{1,17},{9,25... | collective-permute-start | bytes 3932168 | tf_op jit(solution)/shard_map/ppermute | solution.py:188
  97.5 23.2 %all-to-all-done.1 = bf16[32,8,2560]{2,1,0:T(8,128)(2,1)S(1)} async-done(((bf16[32,8,2560]{2,1,0:T(8,128)(2,1)}), bf16[32,8,2560]{2,1,0:T(8,128)(2,1)S(1)}, u32[]{:S(2)}, u32[]{:S(2)}) %all-to-all-start.1) | async-done | bytes 1310752 | tf_op jit(solution)/shard_map/all_to_all | solution.py:199
  120.7 3.4 all-to-all-start
  127.1 22.2 %collective-permute-start.1 = (bf16[256,2560]{1,0:T(8,128)(2,1)S(1)}, bf16[256,2560]{1,0:T(8,128)(2,1)}, u32[]{:S(2)}, u32[]{:S(2)}) collective-permute-start(bf16[256,2560]{1,0:T(8,128)(2,1)S(1)} %bitcast.22), channel_id=1, source_target_pairs={{0,1},{8,9},{2,3},{10,11},{4,5},{12,13},{6,7},{14,15},{1,17},{9,25... | collective-permute-start | bytes 3932168 | tf_op jit(solution)/shard_map/ppermute | solution.py:188
  156.2 17.7 %attend.3 = (bf16[256,2560]{1,0:T(8,128)(2,1)S(1)}, f32[256,2560]{1,0:T(8,128)}, bf16[256,2560]{1,0:T(8,128)(2,1)S(1)}, bf16[256,2560]{1,0:T(8,128)(2,1)S(1)}, b...) custom-call(f32[4]{0:T(128)S(1)} %add_select_fusion.bias_ref, bf16[256,2560]{1,0:T(8,128)(2,1)S(1)} %bitcast.32, ...), custom_call_target="tpu_custom_call" | custom-call | flops 15099494400 | bytes 17039360 | tf_op jit(solution)/shard_map/attend/pallas_call | solution.py:154
  179.2 6.0 %all-to-all-start.5 = ((bf16[32,8,2560]{2,1,0:T(8,128)(2,1)}), bf16[32,8,2560]{2,1,0:T(8,128)(2,1)}, u32[]{:S(2)}, u32[]{:S(2)}) async-start(bf16[32,8,2560]{2,1,0:T(8,128)(2,1)} %bitcast.33), calls=%async_computation.5 | async-start | bytes 2621440 | tf_op jit(solution)/shard_map/all_to_all | solution.py:199
  185.3 17.4 %attend.2 = (bf16[256,2560]{1,0:T(8,128)(2,1)}, f32[256,2560]{1,0:T(8,128)}, bf16[256,2560]{1,0:T(8,128)(2,1)S(1)}, bf16[256,2560]{1,0:T(8,128)(2,1)S(1)}, bf16[...) custom-call(f32[4]{0:T(128)S(1)} %add_select_fusion.bias_ref, bf16[256,2560]{1,0:T(8,128)(2,1)} %bitcast.5.qg_ref, ...), custom_call_target="tpu_custom_call" | custom-call | flops 15099494400 | bytes 17039360 | tf_op jit(solution)/shard_map/attend/pallas_call | solution.py:154
  207.0 11.4 %all-to-all-done.5 = bf16[32,8,2560]{2,1,0:T(8,128)(2,1)} async-done(((bf16[32,8,2560]{2,1,0:T(8,128)(2,1)}), bf16[32,8,2560]{2,1,0:T(8,128)(2,1)}, u32[]{:S(2)}, u32[]{:S(2)}) %all-to-all-start.5) | async-done | bytes 1310752 | tf_op jit(solution)/shard_map/all_to_all | solution.py:199
  218.5 3.6 all-to-all-start.2
  223.3 4.6 %collective-permute-start.14 = (bf16[256,2560]{1,0:T(8,128)(2,1)}, bf16[256,2560]{1,0:T(8,128)(2,1)S(1)}, u32[]{:S(2)}, u32[]{:S(2)}) collective-permute-start(bf16[256,2560]{1,0:T(8,128)(2,1)} %copy-done.15), channel_id=1, source_target_pairs={{0,1},{8,9},{2,3},{10,11},{4,5},{12,13},{6,7},{14,15},{1,17},{9,25... | collective-permute-start | bytes 3932168 | tf_op jit(solution)/shard_map/ppermute | solution.py:188
  232.4 34.4 %collective-permute-done.13 = bf16[256,2560]{1,0:T(8,128)(2,1)S(1)} collective-permute-done((bf16[256,2560]{1,0:T(8,128)(2,1)}, bf16[256,2560]{1,0:T(8,128)(2,1)S(1)}, u32[]{:S(2)}, u32[]{:S(2)}) %collective-permute-start.13) | collective-permute-done | bytes 1310752 | tf_op jit(solution)/shard_map/ppermute | solution.py:188
  266.8 3.6 fusion.1
  270.4 5.2 %all-to-all-start.7 = ((bf16[32,8,2560]{2,1,0:T(8,128)(2,1)}), bf16[32,8,2560]{2,1,0:T(8,128)(2,1)}, u32[]{:S(2)}, u32[]{:S(2)}) async-start(bf16[32,8,2560]{2,1,0:T(8,128)(2,1)} %fusion.1), calls=%async_computation.7 | async-start | bytes 2621440 | tf_op jit(solution)/shard_map/all_to_all | solution.py:199
  275.6 3.7 collective-permute-start.10
  285.0 33.4 %collective-permute-done.10 = bf16[256,2560]{1,0:T(8,128)(2,1)S(1)} collective-permute-done((bf16[256,2560]{1,0:T(8,128)(2,1)}, bf16[256,2560]{1,0:T(8,128)(2,1)S(1)}, u32[]{:S(2)}, u32[]{:S(2)}) %collective-permute-start.10) | collective-permute-done | bytes 1310752 | tf_op jit(solution)/shard_map/ppermute | solution.py:188
  321.4 3.6 fusion
  324.9 6.3 %all-to-all-start.6 = ((bf16[32,8,2560]{2,1,0:T(8,128)(2,1)}), bf16[32,8,2560]{2,1,0:T(8,128)(2,1)S(1)}, u32[]{:S(2)}, u32[]{:S(2)}) async-start(bf16[32,8,2560]{2,1,0:T(8,128)(2,1)} %fusion), calls=%async_computation.6 | async-start | bytes 2621440 | tf_op jit(solution)/shard_map/all_to_all | solution.py:199
  332.1 8.3 %unpack.2 = (bf16[256,2560]{1,0:T(8,128)(2,1)}, bf16[256,2560]{1,0:T(8,128)(2,1)}) custom-call(s32[256,1]{1,0:T(8,128)} %copy.10.landing_ref, bf16[256,2560]{1,0:T(8,128)(2,1)} %bitcast.9.refs_0_, bf16[256,2560]{1,0:T(8,128)(2,1)} %bitcast.15.refs_1_), custom_call_target="tpu_custom_call" | custom-call | flops 671088640 | bytes 5242880 | tf_op jit(solution)/shard_map/unpack/pallas_call | solution.py:95
  340.4 24.1 %all-to-all-done.6 = bf16[32,8,2560]{2,1,0:T(8,128)(2,1)S(1)} async-done(((bf16[32,8,2560]{2,1,0:T(8,128)(2,1)}), bf16[32,8,2560]{2,1,0:T(8,128)(2,1)S(1)}, u32[]{:S(2)}, u32[]{:S(2)}) %all-to-all-start.6) | async-done | bytes 1310752 | tf_op jit(solution)/shard_map/all_to_all | solution.py:199
  365.5 8.3 %unpack.3 = (bf16[256,2560]{1,0:T(8,128)(2,1)}, bf16[256,2560]{1,0:T(8,128)(2,1)}) custom-call(s32[256,1]{1,0:T(8,128)} %copy.10.landing_ref, bf16[256,2560]{1,0:T(8,128)(2,1)} %bitcast.34, bf16[256,2560]{1,0:T(8,128)(2,1)} %bitcast.19.refs_1_), custom_call_target="tpu_custom_call" | custom-call | flops 671088640 | bytes 5242880 | tf_op jit(solution)/shard_map/unpack/pallas_call | solution.py:95
  (76 shorter events, 47.3 us)
Async XLA Ops:
  47.8 35.9 %all-to-all-start.3 = ((bf16[32,8,2560]{2,1,0:T(8,128)(2,1)}), bf16[32,8,2560]{2,1,0:T(8,128)(2,1)S(1)}, u32[]{:S(2)}, u32[]{:S(2)}) async-start(bf16[32,8,2560]{2,1,0:T(8,128)(2,1)} %bitcast.37), calls=%async_computation.3 | async-start | bytes 2621440 | tf_op jit(solution)/shard_map/all_to_all | solution.py:199
  84.8 36.0 %all-to-all-start.1 = ((bf16[32,8,2560]{2,1,0:T(8,128)(2,1)}), bf16[32,8,2560]{2,1,0:T(8,128)(2,1)S(1)}, u32[]{:S(2)}, u32[]{:S(2)}) async-start(bf16[32,8,2560]{2,1,0:T(8,128)(2,1)} %bitcast.36), calls=%async_computation.1 | async-start | bytes 2621440 | tf_op jit(solution)/shard_map/all_to_all | solution.py:199
  87.4 61.9 %collective-permute-start.5 = (bf16[256,2560]{1,0:T(8,128)(2,1)S(1)}, bf16[256,2560]{1,0:T(8,128)(2,1)}, u32[]{:S(2)}, u32[]{:S(2)}) collective-permute-start(bf16[256,2560]{1,0:T(8,128)(2,1)S(1)} %bitcast.27), channel_id=1, source_target_pairs={{0,1},{8,9},{2,3},{10,11},{4,5},{12,13},{6,7},{14,15},{1,17},{9,25... | collective-permute-start | bytes 3932168 | tf_op jit(solution)/shard_map/ppermute | solution.py:188
  92.1 58.6 %collective-permute-start.6 = (bf16[256,2560]{1,0:T(8,128)(2,1)S(1)}, bf16[256,2560]{1,0:T(8,128)(2,1)}, u32[]{:S(2)}, u32[]{:S(2)}) collective-permute-start(bf16[256,2560]{1,0:T(8,128)(2,1)S(1)} %bitcast.28), channel_id=1, source_target_pairs={{1,0},{9,8},{3,2},{11,10},{5,4},{13,12},{7,6},{15,14},{17,1},{25,9... | collective-permute-start | bytes 3932168 | tf_op jit(solution)/shard_map/ppermute | solution.py:188
  93.3 60.2 %collective-permute-start.7 = (bf16[256,2560]{1,0:T(8,128)(2,1)S(1)}, bf16[256,2560]{1,0:T(8,128)(2,1)}, u32[]{:S(2)}, u32[]{:S(2)}) collective-permute-start(bf16[256,2560]{1,0:T(8,128)(2,1)S(1)} %bitcast.29), channel_id=1, source_target_pairs={{0,8},{8,2},{2,10},{10,4},{4,12},{12,6},{6,14},{1,9},{9,3},{3,11},... | collective-permute-start | bytes 3932168 | tf_op jit(solution)/shard_map/ppermute | solution.py:188
  96.2 58.6 %collective-permute-start.8 = (bf16[256,2560]{1,0:T(8,128)(2,1)S(1)}, bf16[256,2560]{1,0:T(8,128)(2,1)}, u32[]{:S(2)}, u32[]{:S(2)}) collective-permute-start(bf16[256,2560]{1,0:T(8,128)(2,1)S(1)} %bitcast.30), channel_id=1, source_target_pairs={{8,0},{2,8},{10,2},{4,10},{12,4},{6,12},{14,6},{9,1},{3,9},{11,3},... | collective-permute-start | bytes 3932168 | tf_op jit(solution)/shard_map/ppermute | solution.py:188
  120.7 58.5 %all-to-all-start = ((bf16[32,8,2560]{2,1,0:T(8,128)(2,1)}), bf16[32,8,2560]{2,1,0:T(8,128)(2,1)}, u32[]{:S(2)}, u32[]{:S(2)}) async-start(bf16[32,8,2560]{2,1,0:T(8,128)(2,1)} %bitcast.35), calls=%async_computation | async-start | bytes 2621440 | tf_op jit(solution)/shard_map/all_to_all | solution.py:199
  124.3 0.8 collective-permute-start
  127.1 58.2 %collective-permute-start.1 = (bf16[256,2560]{1,0:T(8,128)(2,1)S(1)}, bf16[256,2560]{1,0:T(8,128)(2,1)}, u32[]{:S(2)}, u32[]{:S(2)}) collective-permute-start(bf16[256,2560]{1,0:T(8,128)(2,1)S(1)} %bitcast.22), channel_id=1, source_target_pairs={{0,1},{8,9},{2,3},{10,11},{4,5},{12,13},{6,7},{14,15},{1,17},{9,25... | collective-permute-start | bytes 3932168 | tf_op jit(solution)/shard_map/ppermute | solution.py:188
  149.3 35.9 %collective-permute-start.2 = (bf16[256,2560]{1,0:T(8,128)(2,1)S(1)}, bf16[256,2560]{1,0:T(8,128)(2,1)}, u32[]{:S(2)}, u32[]{:S(2)}) collective-permute-start(bf16[256,2560]{1,0:T(8,128)(2,1)S(1)} %bitcast.23), channel_id=1, source_target_pairs={{1,0},{9,8},{3,2},{11,10},{5,4},{13,12},{7,6},{15,14},{17,1},{25,9... | collective-permute-start | bytes 3932168 | tf_op jit(solution)/shard_map/ppermute | solution.py:188
  150.6 34.7 %collective-permute-start.3 = (bf16[256,2560]{1,0:T(8,128)(2,1)S(1)}, bf16[256,2560]{1,0:T(8,128)(2,1)}, u32[]{:S(2)}, u32[]{:S(2)}) collective-permute-start(bf16[256,2560]{1,0:T(8,128)(2,1)S(1)} %bitcast.24), channel_id=1, source_target_pairs={{0,8},{8,2},{2,10},{10,4},{4,12},{12,6},{6,14},{1,9},{9,3},{3,11},... | collective-permute-start | bytes 3932168 | tf_op jit(solution)/shard_map/ppermute | solution.py:188
  153.6 31.7 %collective-permute-start.4 = (bf16[256,2560]{1,0:T(8,128)(2,1)S(1)}, bf16[256,2560]{1,0:T(8,128)(2,1)}, u32[]{:S(2)}, u32[]{:S(2)}) collective-permute-start(bf16[256,2560]{1,0:T(8,128)(2,1)S(1)} %bitcast.25), channel_id=1, source_target_pairs={{8,0},{2,8},{10,2},{4,10},{12,4},{6,12},{14,6},{9,1},{3,9},{11,3},... | collective-permute-start | bytes 3932168 | tf_op jit(solution)/shard_map/ppermute | solution.py:188
  179.2 39.2 %all-to-all-start.5 = ((bf16[32,8,2560]{2,1,0:T(8,128)(2,1)}), bf16[32,8,2560]{2,1,0:T(8,128)(2,1)}, u32[]{:S(2)}, u32[]{:S(2)}) async-start(bf16[32,8,2560]{2,1,0:T(8,128)(2,1)} %bitcast.33), calls=%async_computation.5 | async-start | bytes 2621440 | tf_op jit(solution)/shard_map/all_to_all | solution.py:199
  218.5 51.9 %all-to-all-start.2 = ((bf16[32,8,2560]{2,1,0:T(8,128)(2,1)}), bf16[32,8,2560]{2,1,0:T(8,128)(2,1)}, u32[]{:S(2)}, u32[]{:S(2)}) async-start(bf16[32,8,2560]{2,1,0:T(8,128)(2,1)} %bitcast.8), calls=%async_computation.2 | async-start | bytes 2621440 | tf_op jit(solution)/shard_map/all_to_all | solution.py:199
  222.0 44.8 %collective-permute-start.13 = (bf16[256,2560]{1,0:T(8,128)(2,1)}, bf16[256,2560]{1,0:T(8,128)(2,1)S(1)}, u32[]{:S(2)}, u32[]{:S(2)}) collective-permute-start(bf16[256,2560]{1,0:T(8,128)(2,1)} %copy-done.16), channel_id=1, source_target_pairs={{1,0},{9,8},{3,2},{11,10},{5,4},{13,12},{7,6},{15,14},{17,1},{25,9... | collective-permute-start | bytes 3932168 | tf_op jit(solution)/shard_map/ppermute | solution.py:188
  223.3 43.5 %collective-permute-start.14 = (bf16[256,2560]{1,0:T(8,128)(2,1)}, bf16[256,2560]{1,0:T(8,128)(2,1)S(1)}, u32[]{:S(2)}, u32[]{:S(2)}) collective-permute-start(bf16[256,2560]{1,0:T(8,128)(2,1)} %copy-done.15), channel_id=1, source_target_pairs={{0,1},{8,9},{2,3},{10,11},{4,5},{12,13},{6,7},{14,15},{1,17},{9,25... | collective-permute-start | bytes 3932168 | tf_op jit(solution)/shard_map/ppermute | solution.py:188
  228.0 38.8 %collective-permute-start.15 = (bf16[256,2560]{1,0:T(8,128)(2,1)S(1)}, bf16[256,2560]{1,0:T(8,128)(2,1)S(1)}, u32[]{:S(2)}, u32[]{:S(2)}) collective-permute-start(bf16[256,2560]{1,0:T(8,128)(2,1)S(1)} %copy-done.14), channel_id=1, source_target_pairs={{8,0},{2,8},{10,2},{4,10},{12,4},{6,12},{14,6},{9,1},{3,9},{11,3},... | collective-permute-start | bytes 3932168 | tf_op jit(solution)/shard_map/ppermute | solution.py:188
  229.3 37.5 %collective-permute-start.16 = (bf16[256,2560]{1,0:T(8,128)(2,1)S(1)}, bf16[256,2560]{1,0:T(8,128)(2,1)S(1)}, u32[]{:S(2)}, u32[]{:S(2)}) collective-permute-start(bf16[256,2560]{1,0:T(8,128)(2,1)S(1)} %copy-done.12), channel_id=1, source_target_pairs={{0,8},{8,2},{2,10},{10,4},{4,12},{12,6},{6,14},{1,9},{9,3},{3,11},... | collective-permute-start | bytes 3932168 | tf_op jit(solution)/shard_map/ppermute | solution.py:188
  270.4 54.6 %all-to-all-start.7 = ((bf16[32,8,2560]{2,1,0:T(8,128)(2,1)}), bf16[32,8,2560]{2,1,0:T(8,128)(2,1)}, u32[]{:S(2)}, u32[]{:S(2)}) async-start(bf16[32,8,2560]{2,1,0:T(8,128)(2,1)} %fusion.1), calls=%async_computation.7 | async-start | bytes 2621440 | tf_op jit(solution)/shard_map/all_to_all | solution.py:199
  275.6 42.9 %collective-permute-start.10 = (bf16[256,2560]{1,0:T(8,128)(2,1)}, bf16[256,2560]{1,0:T(8,128)(2,1)S(1)}, u32[]{:S(2)}, u32[]{:S(2)}) collective-permute-start(bf16[256,2560]{1,0:T(8,128)(2,1)} %copy-done.10), channel_id=1, source_target_pairs={{0,1},{8,9},{2,3},{10,11},{4,5},{12,13},{6,7},{14,15},{1,17},{9,25... | collective-permute-start | bytes 3932168 | tf_op jit(solution)/shard_map/ppermute | solution.py:188
  279.3 39.2 %collective-permute-start.11 = (bf16[256,2560]{1,0:T(8,128)(2,1)}, bf16[256,2560]{1,0:T(8,128)(2,1)S(1)}, u32[]{:S(2)}, u32[]{:S(2)}) collective-permute-start(bf16[256,2560]{1,0:T(8,128)(2,1)} %copy-done.9), channel_id=1, source_target_pairs={{8,0},{2,8},{10,2},{4,10},{12,4},{6,12},{14,6},{9,1},{3,9},{11,3},... | collective-permute-start | bytes 3932168 | tf_op jit(solution)/shard_map/ppermute | solution.py:188
  280.6 37.9 %collective-permute-start.12 = (bf16[256,2560]{1,0:T(8,128)(2,1)S(1)}, bf16[256,2560]{1,0:T(8,128)(2,1)S(1)}, u32[]{:S(2)}, u32[]{:S(2)}) collective-permute-start(bf16[256,2560]{1,0:T(8,128)(2,1)S(1)} %copy-done.8), channel_id=1, source_target_pairs={{0,8},{8,2},{2,10},{10,4},{4,12},{12,6},{6,14},{1,9},{9,3},{3,11},... | collective-permute-start | bytes 3932168 | tf_op jit(solution)/shard_map/ppermute | solution.py:188
  283.7 37.6 %collective-permute-start.9 = (bf16[256,2560]{1,0:T(8,128)(2,1)S(1)}, bf16[256,2560]{1,0:T(8,128)(2,1)S(1)}, u32[]{:S(2)}, u32[]{:S(2)}) collective-permute-start(bf16[256,2560]{1,0:T(8,128)(2,1)S(1)} %copy-done.6), channel_id=1, source_target_pairs={{1,0},{9,8},{3,2},{11,10},{5,4},{13,12},{7,6},{15,14},{17,1},{25,9... | collective-permute-start | bytes 3932168 | tf_op jit(solution)/shard_map/ppermute | solution.py:188
  324.9 39.5 %all-to-all-start.6 = ((bf16[32,8,2560]{2,1,0:T(8,128)(2,1)}), bf16[32,8,2560]{2,1,0:T(8,128)(2,1)S(1)}, u32[]{:S(2)}, u32[]{:S(2)}) async-start(bf16[32,8,2560]{2,1,0:T(8,128)(2,1)} %fusion), calls=%async_computation.6 | async-start | bytes 2621440 | tf_op jit(solution)/shard_map/all_to_all | solution.py:199
  (19 other events, 196.1 us)

commit v2 on v1

--- a/solution.py
+++ b/solution.py
@@ -15,7 +15,7 @@
 CHUNKS = 2
 BOTH = ("tm", "space")
 SCALE = HD ** (-0.5)
-VMEM_LIMIT = 40 * 1024 * 1024
+VMEM_LIMIT = 60 * 1024 * 1024
 
 
 def device_of(tile, tm_count, space_count):
@@ -41,70 +41,65 @@
     return lax.dot_general(a, b, (dims, ((), ())), preferred_element_type=jnp.float32)
 
 
-def pack_body(landing_ref, q_ref, k_ref, v_ref, g_ref, kv_ref, qg_ref):
+def pack_body(landing_ref, first_ref, second_ref, *refs):
+    out_ref = refs[-1]
     rows = lax.broadcasted_iota(jnp.int32, (TILE, TILE), 0)
     pick = jnp.where(rows == landing_ref[...], 1.0, 0.0).astype(jnp.bfloat16)
-    for ref, out, at in ((k_ref, kv_ref, 0), (v_ref, kv_ref, 1), (q_ref, qg_ref, 0), (g_ref, qg_ref, 1)):
+    for at, ref in enumerate((first_ref, second_ref)):
         moved = dot(pick, ref[...], ((1,), (0,)))
-        out[:, at * PAIR : (at + 1) * PAIR] = moved.astype(jnp.bfloat16)
-
-
-def pack(landing, arrays, chunk, steps):
+        out_ref[:, at * PAIR : (at + 1) * PAIR] = moved.astype(jnp.bfloat16)
+
+
+def pack(landing, first, second, chunk, steps, after=()):
     width = steps * 2 * PAIR
-    rows = arrays[0].shape[0]
+    rows = first.shape[0]
     source = pl.BlockSpec((rows, PAIR), lambda i: (0, chunk * steps + i))
-    target = pl.BlockSpec((rows, 2 * PAIR), lambda i: (0, i))
-    shape = jax.ShapeDtypeStruct((rows, width), jnp.bfloat16)
     return pl.pallas_call(
         pack_body,
         grid=(steps,),
-        in_specs=[pl.BlockSpec((1, rows), lambda i: (0, 0))] + [source] * 4,
-        out_specs=[target] * 2,
-        out_shape=[shape] * 2,
+        in_specs=[pl.BlockSpec((1, rows), lambda i: (0, 0)), source, source]
+        + [pl.BlockSpec(memory_space=pl.ANY)] * len(after),
+        out_specs=pl.BlockSpec((rows, 2 * PAIR), lambda i: (0, i)),
+        out_shape=jax.ShapeDtypeStruct((rows, width), jnp.bfloat16),
+        compiler_params=pltpu.CompilerParams(vmem_limit_bytes=VMEM_LIMIT),
         cost_estimate=pl.CostEstimate(
-            flops=4 * rows * rows * width, bytes_accessed=8 * rows * width, transcendentals=0
+            flops=2 * rows * rows * width, bytes_accessed=4 * rows * width, transcendentals=0
         ),
         name="pack",
-    )(landing[None, :], *arrays)
-
-
-def unpack_body(steps, landing_ref, *refs):
-    chunk_refs, (first_ref, second_ref) = refs[:-2], refs[-2:]
+    )(landing[None, :], first, second, *after)
+
+
+def unpack_body(landing_ref, moved_ref, *refs):
+    first_ref, second_ref = refs[-2:]
     columns = lax.broadcasted_iota(jnp.int32, (TILE, TILE), 1)
     pick = jnp.where(columns == landing_ref[...], 1.0, 0.0).astype(jnp.bfloat16)
-    step = pl.program_id(0)
-    for chunk, ref in enumerate(chunk_refs):
-
-        @pl.when(step // steps == chunk)
-        def _(ref=ref):
-            moved = dot(pick, ref[...], ((1,), (0,))).astype(jnp.bfloat16)
-            first_ref[...] = moved[:, :PAIR]
-            second_ref[...] = moved[:, PAIR:]
-
-
-def unpack(landing, chunks, steps):
-    rows = chunks[0].shape[0]
-    total = steps * len(chunks)
-    specs = [
-        pl.BlockSpec(
-            (rows, 2 * PAIR), lambda i, c=c: (0, jnp.clip(i - c * steps, 0, steps - 1))
-        )
-        for c in range(len(chunks))
-    ]
-    shape = jax.ShapeDtypeStruct((rows, total * PAIR), jnp.bfloat16)
+    moved = dot(pick, moved_ref[...], ((1,), (0,))).astype(jnp.bfloat16)
+    first_ref[...] = moved[:, :PAIR]
+    second_ref[...] = moved[:, PAIR:]
+
+
+def unpack(landing, moved, before, chunk, steps):
+    rows = moved.shape[0]
+    shape = jax.ShapeDtypeStruct((rows, CHUNKS * steps * PAIR), jnp.bfloat16)
     return pl.pallas_call(
-        functools.partial(unpack_body, steps),
-        grid=(total,),
-        in_specs=[pl.BlockSpec((rows, 1), lambda i: (0, 0))] + specs,
-        out_specs=[pl.BlockSpec((rows, PAIR), lambda i: (0, i))] * 2,
+        unpack_body,
+        grid=(steps,),
+        in_specs=[
+            pl.BlockSpec((rows, 1), lambda i: (0, 0)),
+            pl.BlockSpec((rows, 2 * PAIR), lambda i: (0, i)),
+        ]
+        + [pl.BlockSpec(memory_space=pl.ANY)] * len(before),
+        out_specs=[pl.BlockSpec((rows, PAIR), lambda i: (0, chunk * steps + i))] * 2,
         out_shape=[shape] * 2,
+        input_output_aliases={2 + i: i for i in range(len(before))},
+        compiler_params=pltpu.CompilerParams(vmem_limit_bytes=VMEM_LIMIT),
         cost_estimate=pl.CostEstimate(
-            flops=4 * rows * rows * total * PAIR,
-            bytes_accessed=8 * rows * total * PAIR,
+            flops=4 * rows * rows * steps * PAIR,
+            bytes_accessed=8 * rows * steps * PAIR,
             transcendentals=0,
         ),
         name="unpack",
-    )(landing[:, None], *chunks)
+    )(landing[:, None], moved, *before)
 
 
 def attend_body(bias_ref, qg_ref, *refs):
@@ -199,21 +194,21 @@
         return lax.all_to_all(rows, BOTH, split_axis=0, concat_axis=0, tiled=True)
 
     moves = ((1, 0), (-1, 0), (0, 1), (0, -1))
-    arrays = (query_rows, key_rows, value_rows, out_cotangent)
     back_outputs, back_terms = [], []
     for chunk in range(CHUNKS):
-        send_kv, send_qg = pack(landing, arrays, chunk, steps)
-        kv = exchange(send_kv)
-        qg = exchange(send_qg)
+        kv = exchange(pack(landing, key_rows, value_rows, chunk, steps))
+        qg = exchange(pack(landing, query_rows, out_cotangent, chunk, steps))
         kvs = [kv] + [passed(kv, *move) for move in moves]
         outputs, own, *sides = attend(bias, qg, kvs, steps)
         back_outputs.append(exchange(outputs))
         terms = [passed(side, -a, -b) for side, (a, b) in zip(sides, moves)]
         total = own + sum(term.astype(jnp.float32) for term in terms)
         back_terms.append(exchange(total.astype(jnp.bfloat16)))
-    attended, query_grad = unpack(landing, back_outputs, steps)
-    key_grad, value_grad = unpack(landing, back_terms, steps)
-    return (attended, query_grad, key_grad, value_grad)
+    output_pair, term_pair = (), ()
+    for chunk in range(CHUNKS):
+        output_pair = unpack(landing, back_outputs[chunk], output_pair, chunk, steps)
+        term_pair = unpack(landing, back_terms[chunk], term_pair, chunk, steps)
+    return (*output_pair, *term_pair)
 
 
 def solution(mesh):

time: 376 us -> 370 us (0.984)
  blocking collectives: 40.5 us -> 0 us
  waiting for transfers between devices: 157 us -> 177 us
  starting transfers between devices: 87.9 us -> 101 us
  Pallas kernels: 62.6 us -> 71.9 us
  local copies, waits for them, and re-layouts: 14.7 us -> 5.94 us
    all_to_all x1 -> x0, blocking collectives: 40.5 us -> none  [exchange(): return lax.all_to_all(rows, BOTH, split_axis=0, concat_axis=0, tiled=True)]
    ppermute x16, waiting for transfers between devices: 70.7 us -> 81.1 us  [passed(): return lax.ppermute(block, BOTH, pairs)]
    all_to_all x7 -> x8, waiting for transfers between devices: 86.5 us -> 95.8 us  [exchange(): return lax.all_to_all(rows, BOTH, split_axis=0, concat_axis=0, tiled=True)]
    unnamed x38 -> x18, local copies, waits for them, and re-layouts: 13.1 us -> 4.38 us
    pallas_call x2 -> x4, Pallas kernels: 10.8 us -> 18.3 us  [pack(): pl.pallas_call(pack_body, grid=(steps,), in_specs=[pl.BlockSpec((1, rows)...]
    ppermute x16, starting transfers between devices: 57.5 us -> 64.8 us  [passed(): return lax.ppermute(block, BOTH, pairs)]
    all_to_all x7 -> x8, starting transfers between devices: 29.8 us -> 36 us  [exchange(): return lax.all_to_all(rows, BOTH, split_axis=0, concat_axis=0, tiled=True)]
    pallas_call x2 -> x4, Pallas kernels: 16.6 us -> 18.5 us  [unpack(): pl.pallas_call(unpack_body, grid=(steps,), in_specs=[pl.BlockSpec((rows,...]
  transfers between devices with their start and end apart: 24 -> 25, of which waited for: 7 -> 9; matrix products, arithmetic and copies ran while one was open for 2% -> 3% of each run, Pallas kernels for 13% -> 17%
where the time goes in v2:
time: 370 us; the launch traced here: 368 us
  waiting for transfers between devices  177 us (48%)
  starting transfers between devices  101 us (27%)
  Pallas kernels  71.9 us (19%)
  other arithmetic  9.13 us (2%)
  local copies, waits for them, and re-layouts  5.94 us (2%)
    all_to_all x8, waiting for transfers between devices, exchange(): return lax.all_to_all(rows, BOTH, split_axis=0, concat_axis=0, tiled=True)  95.8 us
    ppermute x16, waiting for transfers between devices, passed(): return lax.ppermute(block, BOTH, pairs)  81.1 us
    ppermute x16, starting transfers between devices, passed(): return lax.ppermute(block, BOTH, pairs)  64.8 us
    all_to_all x8, starting transfers between devices, exchange(): return lax.all_to_all(rows, BOTH, split_axis=0, concat_axis=0, tiled=True)  36 us
    pallas_call x2, Pallas kernels, attend(): pl.pallas_call(attend_body, grid=(steps,), in_specs=[pl.BlockSpec(memory_...  35.1 us
    pallas_call x4, Pallas kernels, unpack(): pl.pallas_call(unpack_body, grid=(steps,), in_specs=[pl.BlockSpec((rows,...  18.5 us
    pallas_call x4, Pallas kernels, pack(): pl.pallas_call(pack_body, grid=(steps,), in_specs=[pl.BlockSpec((1, rows)...  18.3 us
  transfers between devices with their start and end apart: 25, of which 9 were waited for; matrix products, arithmetic and copies ran while one was open for 3% of the time, Pallas kernels for 17%

profile of v2, /device:TPU:0, one launch (start us, length us, event | category | flops | bytes accessed | tf_op | source)
XLA Modules:
  0.0 367.6 jit_solution(14682420917227121210)
XLA Ops:
  6.5 7.3 %all-to-all-start.4 = ((bf16[32,8,2560]{2,1,0:T(8,128)(2,1)}), bf16[32,8,2560]{2,1,0:T(8,128)(2,1)S(1)}, u32[]{:S(2)}, u32[]{:S(2)}) async-start(bf16[32,8,2560]{2,1,0:T(8,128)(2,1)} %bitcast.29), calls=%async_computation.4 | async-start | bytes 2621440 | tf_op jit(solution)/shard_map/all_to_all | solution.py:194
  18.4 28.6 %all-to-all-done.4 = bf16[32,8,2560]{2,1,0:T(8,128)(2,1)S(1)} async-done(((bf16[32,8,2560]{2,1,0:T(8,128)(2,1)}), bf16[32,8,2560]{2,1,0:T(8,128)(2,1)S(1)}, u32[]{:S(2)}, u32[]{:S(2)}) %all-to-all-start.4) | async-done | bytes 1310752 | tf_op jit(solution)/shard_map/all_to_all | solution.py:194
  54.2 28.6 %all-to-all-done.1 = bf16[32,8,2560]{2,1,0:T(8,128)(2,1)S(1)} async-done(((bf16[32,8,2560]{2,1,0:T(8,128)(2,1)}), bf16[32,8,2560]{2,1,0:T(8,128)(2,1)S(1)}, u32[]{:S(2)}, u32[]{:S(2)}) %all-to-all-start.1) | async-done | bytes 1310752 | tf_op jit(solution)/shard_map/all_to_all | solution.py:194
  93.0 5.7 %collective-permute-start.1 = (bf16[256,2560]{1,0:T(8,128)(2,1)S(1)}, bf16[256,2560]{1,0:T(8,128)(2,1)}, u32[]{:S(2)}, u32[]{:S(2)}) collective-permute-start(bf16[256,2560]{1,0:T(8,128)(2,1)S(1)} %bitcast.38), channel_id=1, source_target_pairs={{0,1},{8,9},{2,3},{10,11},{4,5},{12,13},{6,7},{14,15},{1,17},{9,25... | collective-permute-start | bytes 3932168 | tf_op jit(solution)/shard_map/ppermute | solution.py:183
  98.7 4.6 %pack.6 = bf16[256,2560]{1,0:T(8,128)(2,1)} custom-call(s32[1,256]{1,0:T(1,128)} %bitcast.45, bf16[256,2560]{1,0:T(8,128)(2,1)} %first_ref.6, bf16[256,2560]{1,0:T(8,128)(2,1)} %second_ref.6), custom_call_target="tpu_custom_call" | custom-call | flops 335544320 | bytes 2621440 | tf_op jit(solution)/shard_map/pack/pallas_call | solution.py:57
  103.3 16.2 %all-to-all-done = bf16[32,8,2560]{2,1,0:T(8,128)(2,1)} async-done(((bf16[32,8,2560]{2,1,0:T(8,128)(2,1)}), bf16[32,8,2560]{2,1,0:T(8,128)(2,1)}, u32[]{:S(2)}, u32[]{:S(2)}) %all-to-all-start) | async-done | bytes 1310752 | tf_op jit(solution)/shard_map/all_to_all | solution.py:194
  127.6 23.6 %collective-permute-start.7 = (bf16[256,2560]{1,0:T(8,128)(2,1)S(1)}, bf16[256,2560]{1,0:T(8,128)(2,1)}, u32[]{:S(2)}, u32[]{:S(2)}) collective-permute-start(bf16[256,2560]{1,0:T(8,128)(2,1)S(1)} %bitcast.31), channel_id=1, source_target_pairs={{0,8},{8,2},{2,10},{10,4},{4,12},{12,6},{6,14},{1,9},{9,3},{3,11},... | collective-permute-start | bytes 3932168 | tf_op jit(solution)/shard_map/ppermute | solution.py:183
  152.5 5.6 %collective-permute-start.5 = (bf16[256,2560]{1,0:T(8,128)(2,1)S(1)}, bf16[256,2560]{1,0:T(8,128)(2,1)}, u32[]{:S(2)}, u32[]{:S(2)}) collective-permute-start(bf16[256,2560]{1,0:T(8,128)(2,1)S(1)} %bitcast.33), channel_id=1, source_target_pairs={{0,1},{8,9},{2,3},{10,11},{4,5},{12,13},{6,7},{14,15},{1,17},{9,25... | collective-permute-start | bytes 3932168 | tf_op jit(solution)/shard_map/ppermute | solution.py:183
  158.1 17.5 %attend.2 = (bf16[256,2560]{1,0:T(8,128)(2,1)}, f32[256,2560]{1,0:T(8,128)}, bf16[256,2560]{1,0:T(8,128)(2,1)}, bf16[256,2560]{1,0:T(8,128)(2,1)}, bf16[256,2560]{1,0:T(8,128)(2,1)}, /*index=5*/bf16[256,2560]{1,0:T(8,128)(2,1)}) custom-call(f32[4]{0:T(128)} %add_select_fusion.bias_ref, bf16[256,2560]{1,0:T(8,128)(2,1)} %bitcast.5.qg_ref, ...), custom_call_target="tpu_custom_call" | custom-call | flops 15099494400 | bytes 17039360 | tf_op jit(solution)/shard_map/attend/pallas_call | solution.py:149
  175.6 5.2 %all-to-all-start.2 = ((bf16[32,8,2560]{2,1,0:T(8,128)(2,1)}), bf16[32,8,2560]{2,1,0:T(8,128)(2,1)S(1)}, u32[]{:S(2)}, u32[]{:S(2)}) async-start(bf16[32,8,2560]{2,1,0:T(8,128)(2,1)} %bitcast.41), calls=%async_computation.2 | async-start | bytes 2621440 | tf_op jit(solution)/shard_map/all_to_all | solution.py:194
  180.8 5.7 %collective-permute-done.6.refs_2_ = bf16[256,2560]{1,0:T(8,128)(2,1)} collective-permute-done((bf16[256,2560]{1,0:T(8,128)(2,1)S(1)}, bf16[256,2560]{1,0:T(8,128)(2,1)}, u32[]{:S(2)}, u32[]{:S(2)}) %collective-permute-start.6) | collective-permute-done | bytes 1310752 | tf_op jit(solution)/shard_map/ppermute | solution.py:183
  186.5 6.0 %collective-permute-done.5.refs_1_ = bf16[256,2560]{1,0:T(8,128)(2,1)} collective-permute-done((bf16[256,2560]{1,0:T(8,128)(2,1)S(1)}, bf16[256,2560]{1,0:T(8,128)(2,1)}, u32[]{:S(2)}, u32[]{:S(2)}) %collective-permute-start.5) | collective-permute-done | bytes 1310752 | tf_op jit(solution)/shard_map/ppermute | solution.py:183
  192.5 17.6 %attend.3 = (bf16[256,2560]{1,0:T(8,128)(2,1)}, f32[256,2560]{1,0:T(8,128)}, bf16[256,2560]{1,0:T(8,128)(2,1)}, bf16[256,2560]{1,0:T(8,128)(2,1)}, bf16[256,2560]{1,0:T(8,128)(2,1)}, /*index=5*/bf16[256,2560]{1,0:T(8,128)(2,1)}) custom-call(f32[4]{0:T(128)} %add_select_fusion.bias_ref, bf16[256,2560]{1,0:T(8,128)(2,1)} %bitcast.11.qg_ref, ...), custom_call_target="tpu_custom_call" | custom-call | flops 15099494400 | bytes 17039360 | tf_op jit(solution)/shard_map/attend/pallas_call | solution.py:149
  220.5 4.6 %collective-permute-start.14 = (bf16[256,2560]{1,0:T(8,128)(2,1)}, bf16[256,2560]{1,0:T(8,128)(2,1)S(1)}, u32[]{:S(2)}, u32[]{:S(2)}) collective-permute-start(bf16[256,2560]{1,0:T(8,128)(2,1)} %get-tuple-element.37), channel_id=1, source_target_pairs={{0,1},{8,9},{2,3},{10,11},{4,5},{12,13},{6,7},{14,15},{1,17},{9,25... | collective-permute-start | bytes 3932168 | tf_op jit(solution)/shard_map/ppermute | solution.py:183
  229.5 34.6 %collective-permute-done.13 = bf16[256,2560]{1,0:T(8,128)(2,1)S(1)} collective-permute-done((bf16[256,2560]{1,0:T(8,128)(2,1)}, bf16[256,2560]{1,0:T(8,128)(2,1)S(1)}, u32[]{:S(2)}, u32[]{:S(2)}) %collective-permute-start.13) | collective-permute-done | bytes 1310752 | tf_op jit(solution)/shard_map/ppermute | solution.py:183
  268.9 5.0 %all-to-all-start.7 = ((bf16[32,8,2560]{2,1,0:T(8,128)(2,1)}), bf16[32,8,2560]{2,1,0:T(8,128)(2,1)S(1)}, u32[]{:S(2)}, u32[]{:S(2)}) async-start(bf16[32,8,2560]{2,1,0:T(8,128)(2,1)} %fusion.1), calls=%async_computation.7 | async-start | bytes 2621440 | tf_op jit(solution)/shard_map/all_to_all | solution.py:194
  275.2 4.6 %collective-permute-start.10 = (bf16[256,2560]{1,0:T(8,128)(2,1)}, bf16[256,2560]{1,0:T(8,128)(2,1)S(1)}, u32[]{:S(2)}, u32[]{:S(2)}) collective-permute-start(bf16[256,2560]{1,0:T(8,128)(2,1)} %get-tuple-element.32), channel_id=1, source_target_pairs={{0,1},{8,9},{2,3},{10,11},{4,5},{12,13},{6,7},{14,15},{1,17},{9,25... | collective-permute-start | bytes 3932168 | tf_op jit(solution)/shard_map/ppermute | solution.py:183
  284.3 34.6 %collective-permute-done.9 = bf16[256,2560]{1,0:T(8,128)(2,1)S(1)} collective-permute-done((bf16[256,2560]{1,0:T(8,128)(2,1)}, bf16[256,2560]{1,0:T(8,128)(2,1)S(1)}, u32[]{:S(2)}, u32[]{:S(2)}) %collective-permute-start.9) | collective-permute-done | bytes 1310752 | tf_op jit(solution)/shard_map/ppermute | solution.py:183
  323.6 5.0 %all-to-all-start.6 = ((bf16[32,8,2560]{2,1,0:T(8,128)(2,1)}), bf16[32,8,2560]{2,1,0:T(8,128)(2,1)S(1)}, u32[]{:S(2)}, u32[]{:S(2)}) async-start(bf16[32,8,2560]{2,1,0:T(8,128)(2,1)} %fusion), calls=%async_computation.6 | async-start | bytes 2621440 | tf_op jit(solution)/shard_map/all_to_all | solution.py:194
  329.5 4.6 %unpack.4 = (bf16[256,2560]{1,0:T(8,128)(2,1)}, bf16[256,2560]{1,0:T(8,128)(2,1)}) custom-call(s32[256,1]{1,0:T(8,128)} %copy.15.landing_ref, bf16[256,2560]{1,0:T(8,128)(2,1)} %bitcast.24), custom_call_target="tpu_custom_call" | custom-call | flops 335544320 | bytes 2621440 | tf_op jit(solution)/shard_map/unpack/pallas_call | solution.py:84
  334.1 4.6 %unpack.5 = (bf16[256,2560]{1,0:T(8,128)(2,1)}, bf16[256,2560]{1,0:T(8,128)(2,1)}) custom-call(s32[256,1]{1,0:T(8,128)} %copy.15.landing_ref, bf16[256,2560]{1,0:T(8,128)(2,1)} %bitcast.23, bf16[256,2560]{1,0:T(8,128)(2,1)} %get-tuple-element.26.refs_0_, bf16[256,2560]{1,0:T(8,128)(2,1)} %get-tuple-element.27.refs_1_), custom_call_target="tpu_custom_call", output_to_operand_aliasing={{0}: (2, {}), {1}: (3, {})} | custom-call | flops 335544320 | bytes 2621440 | tf_op jit(solution)/shard_map/unpack/pallas_call | solution.py:84
  338.7 4.6 %unpack.6 = (bf16[256,2560]{1,0:T(8,128)(2,1)}, bf16[256,2560]{1,0:T(8,128)(2,1)}) custom-call(s32[256,1]{1,0:T(8,128)} %copy.15.landing_ref, bf16[256,2560]{1,0:T(8,128)(2,1)} %bitcast.25), custom_call_target="tpu_custom_call" | custom-call | flops 335544320 | bytes 2621440 | tf_op jit(solution)/shard_map/unpack/pallas_call | solution.py:84
  343.4 18.5 %all-to-all-done.6 = bf16[32,8,2560]{2,1,0:T(8,128)(2,1)S(1)} async-done(((bf16[32,8,2560]{2,1,0:T(8,128)(2,1)}), bf16[32,8,2560]{2,1,0:T(8,128)(2,1)S(1)}, u32[]{:S(2)}, u32[]{:S(2)}) %all-to-all-start.6) | async-done | bytes 1310752 | tf_op jit(solution)/shard_map/all_to_all | solution.py:194
  363.0 4.6 %unpack.7 = (bf16[256,2560]{1,0:T(8,128)(2,1)}, bf16[256,2560]{1,0:T(8,128)(2,1)}) custom-call(s32[256,1]{1,0:T(8,128)} %copy.15.landing_ref, bf16[256,2560]{1,0:T(8,128)(2,1)} %bitcast.26, bf16[256,2560]{1,0:T(8,128)(2,1)} %get-tuple-element.40.refs_0_, bf16[256,2560]{1,0:T(8,128)(2,1)} %get-tuple-element.41.refs_1_), custom_call_target="tpu_custom_call", output_to_operand_aliasing={{0}: (2, {}), {1}: (3, {})} | custom-call | flops 335544320 | bytes 2621440 | tf_op jit(solution)/shard_map/unpack/pallas_call | solution.py:84
  (61 shorter events, 67.6 us)
Async XLA Ops:
  6.5 40.5 %all-to-all-start.4 = ((bf16[32,8,2560]{2,1,0:T(8,128)(2,1)}), bf16[32,8,2560]{2,1,0:T(8,128)(2,1)S(1)}, u32[]{:S(2)}, u32[]{:S(2)}) async-start(bf16[32,8,2560]{2,1,0:T(8,128)(2,1)} %bitcast.29), calls=%async_computation.4 | async-start | bytes 2621440 | tf_op jit(solution)/shard_map/all_to_all | solution.py:194
  47.0 35.9 %all-to-all-start.1 = ((bf16[32,8,2560]{2,1,0:T(8,128)(2,1)}), bf16[32,8,2560]{2,1,0:T(8,128)(2,1)S(1)}, u32[]{:S(2)}, u32[]{:S(2)}) async-start(bf16[32,8,2560]{2,1,0:T(8,128)(2,1)} %bitcast.28), calls=%async_computation.1 | async-start | bytes 2621440 | tf_op jit(solution)/shard_map/all_to_all | solution.py:194
  82.9 36.6 %all-to-all-start = ((bf16[32,8,2560]{2,1,0:T(8,128)(2,1)}), bf16[32,8,2560]{2,1,0:T(8,128)(2,1)}, u32[]{:S(2)}, u32[]{:S(2)}) async-start(bf16[32,8,2560]{2,1,0:T(8,128)(2,1)} %bitcast.27), calls=%async_computation | async-start | bytes 2621440 | tf_op jit(solution)/shard_map/all_to_all | solution.py:194
  86.3 41.3 %collective-permute-start.4 = (bf16[256,2560]{1,0:T(8,128)(2,1)S(1)}, bf16[256,2560]{1,0:T(8,128)(2,1)}, u32[]{:S(2)}, u32[]{:S(2)}) collective-permute-start(bf16[256,2560]{1,0:T(8,128)(2,1)S(1)} %bitcast.35), channel_id=1, source_target_pairs={{8,0},{2,8},{10,2},{4,10},{12,4},{6,12},{14,6},{9,1},{3,9},{11,3},... | collective-permute-start | bytes 3932168 | tf_op jit(solution)/shard_map/ppermute | solution.py:183
  87.6 63.6 %collective-permute-start.3 = (bf16[256,2560]{1,0:T(8,128)(2,1)S(1)}, bf16[256,2560]{1,0:T(8,128)(2,1)}, u32[]{:S(2)}, u32[]{:S(2)}) collective-permute-start(bf16[256,2560]{1,0:T(8,128)(2,1)S(1)} %bitcast.36), channel_id=1, source_target_pairs={{0,8},{8,2},{2,10},{10,4},{4,12},{12,6},{6,14},{1,9},{9,3},{3,11},... | collective-permute-start | bytes 3932168 | tf_op jit(solution)/shard_map/ppermute | solution.py:183
  91.7 60.7 %collective-permute-start.2 = (bf16[256,2560]{1,0:T(8,128)(2,1)S(1)}, bf16[256,2560]{1,0:T(8,128)(2,1)}, u32[]{:S(2)}, u32[]{:S(2)}) collective-permute-start(bf16[256,2560]{1,0:T(8,128)(2,1)S(1)} %bitcast.37), channel_id=1, source_target_pairs={{1,0},{9,8},{3,2},{11,10},{5,4},{13,12},{7,6},{15,14},{17,1},{25,9... | collective-permute-start | bytes 3932168 | tf_op jit(solution)/shard_map/ppermute | solution.py:183
  93.0 65.1 %collective-permute-start.1 = (bf16[256,2560]{1,0:T(8,128)(2,1)S(1)}, bf16[256,2560]{1,0:T(8,128)(2,1)}, u32[]{:S(2)}, u32[]{:S(2)}) collective-permute-start(bf16[256,2560]{1,0:T(8,128)(2,1)S(1)} %bitcast.38), channel_id=1, source_target_pairs={{0,1},{8,9},{2,3},{10,11},{4,5},{12,13},{6,7},{14,15},{1,17},{9,25... | collective-permute-start | bytes 3932168 | tf_op jit(solution)/shard_map/ppermute | solution.py:183
  119.5 56.1 %all-to-all-start.3 = ((bf16[32,8,2560]{2,1,0:T(8,128)(2,1)}), bf16[32,8,2560]{2,1,0:T(8,128)(2,1)}, u32[]{:S(2)}, u32[]{:S(2)}) async-start(bf16[32,8,2560]{2,1,0:T(8,128)(2,1)} %bitcast.22), calls=%async_computation.3 | async-start | bytes 2621440 | tf_op jit(solution)/shard_map/all_to_all | solution.py:194
  126.3 54.5 %collective-permute-start.8 = (bf16[256,2560]{1,0:T(8,128)(2,1)S(1)}, bf16[256,2560]{1,0:T(8,128)(2,1)}, u32[]{:S(2)}, u32[]{:S(2)}) collective-permute-start(bf16[256,2560]{1,0:T(8,128)(2,1)S(1)} %bitcast.30), channel_id=1, source_target_pairs={{8,0},{2,8},{10,2},{4,10},{12,4},{6,12},{14,6},{9,1},{3,9},{11,3},... | collective-permute-start | bytes 3932168 | tf_op jit(solution)/shard_map/ppermute | solution.py:183
  127.6 53.2 %collective-permute-start.7 = (bf16[256,2560]{1,0:T(8,128)(2,1)S(1)}, bf16[256,2560]{1,0:T(8,128)(2,1)}, u32[]{:S(2)}, u32[]{:S(2)}) collective-permute-start(bf16[256,2560]{1,0:T(8,128)(2,1)S(1)} %bitcast.31), channel_id=1, source_target_pairs={{0,8},{8,2},{2,10},{10,4},{4,12},{12,6},{6,14},{1,9},{9,3},{3,11},... | collective-permute-start | bytes 3932168 | tf_op jit(solution)/shard_map/ppermute | solution.py:183
  151.1 35.3 %collective-permute-start.6 = (bf16[256,2560]{1,0:T(8,128)(2,1)S(1)}, bf16[256,2560]{1,0:T(8,128)(2,1)}, u32[]{:S(2)}, u32[]{:S(2)}) collective-permute-start(bf16[256,2560]{1,0:T(8,128)(2,1)S(1)} %bitcast.32), channel_id=1, source_target_pairs={{1,0},{9,8},{3,2},{11,10},{5,4},{13,12},{7,6},{15,14},{17,1},{25,9... | collective-permute-start | bytes 3932168 | tf_op jit(solution)/shard_map/ppermute | solution.py:183
  152.5 40.1 %collective-permute-start.5 = (bf16[256,2560]{1,0:T(8,128)(2,1)S(1)}, bf16[256,2560]{1,0:T(8,128)(2,1)}, u32[]{:S(2)}, u32[]{:S(2)}) collective-permute-start(bf16[256,2560]{1,0:T(8,128)(2,1)S(1)} %bitcast.33), channel_id=1, source_target_pairs={{0,1},{8,9},{2,3},{10,11},{4,5},{12,13},{6,7},{14,15},{1,17},{9,25... | collective-permute-start | bytes 3932168 | tf_op jit(solution)/shard_map/ppermute | solution.py:183
  175.6 38.4 %all-to-all-start.2 = ((bf16[32,8,2560]{2,1,0:T(8,128)(2,1)}), bf16[32,8,2560]{2,1,0:T(8,128)(2,1)S(1)}, u32[]{:S(2)}, u32[]{:S(2)}) async-start(bf16[32,8,2560]{2,1,0:T(8,128)(2,1)} %bitcast.41), calls=%async_computation.2 | async-start | bytes 2621440 | tf_op jit(solution)/shard_map/all_to_all | solution.py:194
  215.0 52.8 %all-to-all-start.5 = ((bf16[32,8,2560]{2,1,0:T(8,128)(2,1)}), bf16[32,8,2560]{2,1,0:T(8,128)(2,1)S(1)}, u32[]{:S(2)}, u32[]{:S(2)}) async-start(bf16[32,8,2560]{2,1,0:T(8,128)(2,1)} %bitcast.40), calls=%async_computation.5 | async-start | bytes 2621440 | tf_op jit(solution)/shard_map/all_to_all | solution.py:194
  219.2 45.0 %collective-permute-start.13 = (bf16[256,2560]{1,0:T(8,128)(2,1)}, bf16[256,2560]{1,0:T(8,128)(2,1)S(1)}, u32[]{:S(2)}, u32[]{:S(2)}) collective-permute-start(bf16[256,2560]{1,0:T(8,128)(2,1)} %get-tuple-element.36), channel_id=1, source_target_pairs={{1,0},{9,8},{3,2},{11,10},{5,4},{13,12},{7,6},{15,14},{17,1},{25,9... | collective-permute-start | bytes 3932168 | tf_op jit(solution)/shard_map/ppermute | solution.py:183
  220.5 43.7 %collective-permute-start.14 = (bf16[256,2560]{1,0:T(8,128)(2,1)}, bf16[256,2560]{1,0:T(8,128)(2,1)S(1)}, u32[]{:S(2)}, u32[]{:S(2)}) collective-permute-start(bf16[256,2560]{1,0:T(8,128)(2,1)} %get-tuple-element.37), channel_id=1, source_target_pairs={{0,1},{8,9},{2,3},{10,11},{4,5},{12,13},{6,7},{14,15},{1,17},{9,25... | collective-permute-start | bytes 3932168 | tf_op jit(solution)/shard_map/ppermute | solution.py:183
  225.1 39.1 %collective-permute-start.15 = (bf16[256,2560]{1,0:T(8,128)(2,1)}, bf16[256,2560]{1,0:T(8,128)(2,1)S(1)}, u32[]{:S(2)}, u32[]{:S(2)}) collective-permute-start(bf16[256,2560]{1,0:T(8,128)(2,1)} %get-tuple-element.38), channel_id=1, source_target_pairs={{8,0},{2,8},{10,2},{4,10},{12,4},{6,12},{14,6},{9,1},{3,9},{11,3},... | collective-permute-start | bytes 3932168 | tf_op jit(solution)/shard_map/ppermute | solution.py:183
  226.4 37.8 %collective-permute-start.16 = (bf16[256,2560]{1,0:T(8,128)(2,1)}, bf16[256,2560]{1,0:T(8,128)(2,1)S(1)}, u32[]{:S(2)}, u32[]{:S(2)}) collective-permute-start(bf16[256,2560]{1,0:T(8,128)(2,1)} %get-tuple-element.39), channel_id=1, source_target_pairs={{0,8},{8,2},{2,10},{10,4},{4,12},{12,6},{6,14},{1,9},{9,3},{3,11},... | collective-permute-start | bytes 3932168 | tf_op jit(solution)/shard_map/ppermute | solution.py:183
  268.9 53.6 %all-to-all-start.7 = ((bf16[32,8,2560]{2,1,0:T(8,128)(2,1)}), bf16[32,8,2560]{2,1,0:T(8,128)(2,1)S(1)}, u32[]{:S(2)}, u32[]{:S(2)}) async-start(bf16[32,8,2560]{2,1,0:T(8,128)(2,1)} %fusion.1), calls=%async_computation.7 | async-start | bytes 2621440 | tf_op jit(solution)/shard_map/all_to_all | solution.py:194
  273.9 45.0 %collective-permute-start.9 = (bf16[256,2560]{1,0:T(8,128)(2,1)}, bf16[256,2560]{1,0:T(8,128)(2,1)S(1)}, u32[]{:S(2)}, u32[]{:S(2)}) collective-permute-start(bf16[256,2560]{1,0:T(8,128)(2,1)} %get-tuple-element.31), channel_id=1, source_target_pairs={{1,0},{9,8},{3,2},{11,10},{5,4},{13,12},{7,6},{15,14},{17,1},{25,9... | collective-permute-start | bytes 3932168 | tf_op jit(solution)/shard_map/ppermute | solution.py:183
  275.2 43.7 %collective-permute-start.10 = (bf16[256,2560]{1,0:T(8,128)(2,1)}, bf16[256,2560]{1,0:T(8,128)(2,1)S(1)}, u32[]{:S(2)}, u32[]{:S(2)}) collective-permute-start(bf16[256,2560]{1,0:T(8,128)(2,1)} %get-tuple-element.32), channel_id=1, source_target_pairs={{0,1},{8,9},{2,3},{10,11},{4,5},{12,13},{6,7},{14,15},{1,17},{9,25... | collective-permute-start | bytes 3932168 | tf_op jit(solution)/shard_map/ppermute | solution.py:183
  279.8 39.1 %collective-permute-start.11 = (bf16[256,2560]{1,0:T(8,128)(2,1)}, bf16[256,2560]{1,0:T(8,128)(2,1)S(1)}, u32[]{:S(2)}, u32[]{:S(2)}) collective-permute-start(bf16[256,2560]{1,0:T(8,128)(2,1)} %get-tuple-element.33), channel_id=1, source_target_pairs={{8,0},{2,8},{10,2},{4,10},{12,4},{6,12},{14,6},{9,1},{3,9},{11,3},... | collective-permute-start | bytes 3932168 | tf_op jit(solution)/shard_map/ppermute | solution.py:183
  281.1 37.8 %collective-permute-start.12 = (bf16[256,2560]{1,0:T(8,128)(2,1)}, bf16[256,2560]{1,0:T(8,128)(2,1)S(1)}, u32[]{:S(2)}, u32[]{:S(2)}) collective-permute-start(bf16[256,2560]{1,0:T(8,128)(2,1)} %get-tuple-element.34), channel_id=1, source_target_pairs={{0,8},{8,2},{2,10},{10,4},{4,12},{12,6},{6,14},{1,9},{9,3},{3,11},... | collective-permute-start | bytes 3932168 | tf_op jit(solution)/shard_map/ppermute | solution.py:183
  323.6 38.2 %all-to-all-start.6 = ((bf16[32,8,2560]{2,1,0:T(8,128)(2,1)}), bf16[32,8,2560]{2,1,0:T(8,128)(2,1)S(1)}, u32[]{:S(2)}, u32[]{:S(2)}) async-start(bf16[32,8,2560]{2,1,0:T(8,128)(2,1)} %fusion), calls=%async_computation.6 | async-start | bytes 2621440 | tf_op jit(solution)/shard_map/all_to_all | solution.py:194
  (10 other events, 254.9 us)
